TPU v7x, 256 devices: a whole 4x4x8 slice. The times are simulated.
256 devices in a mesh: chan: 128 (over x_hi, y, z, core), tm: 2 (over x_lo).
Axes of the slice: x: 4 (x_hi: 2, x_lo: 2; x = x_hi * 2 + x_lo), y: 4, z: 8, core: 2. Of those that a mesh axis runs over, the one named last changes fastest.
Arguments:
- signal: bfloat16 [16384, 6144], P('chan', 'tm'), may hold values from -6 to 6
- fan_mask: int32 [128, 128], replicated, may hold values 0 or 1
Outputs:
- filtered: bfloat16 [16384, 6144], P('chan', 'tm')
All inputs are finite; a program needn't handle non-finite values.
Results may differ from a plain program's by a relative error of at most 0.0063.
Values may be sent and summed in bfloat16 or wider, within the bound.
A program may use at most 64 MiB of HBM per device.

v0:
```python
import math

import jax
import jax.numpy as jnp
from jax import lax
from jax.sharding import PartitionSpec as P

WINDOW = 4096
BAND = 512
BIN_TILE = 4
WAVE_TILE = 128


def partner_2(array, axis, distance):
    return lax.ppermute(array, axis, [(i, i ^ 1 << distance) for i in range(lax.axis_size(axis))])


def time_tables():
    positions = jnp.arange(WINDOW, dtype=jnp.int32)
    bin_index = jnp.arange(BAND, dtype=jnp.int32)
    product = positions[:, None] * bin_index[None, :] % WINDOW
    phase_angle = 2.0 * math.pi / WINDOW * product.astype(jnp.float32)
    forward = jnp.concatenate([jnp.cos(phase_angle), -jnp.sin(phase_angle)], axis=1).astype(
        jnp.bfloat16
    )
    weight = jnp.where(bin_index == 0, 1.0, 2.0).astype(jnp.float32)
    inverse = jnp.concatenate(
        [weight[:, None] * jnp.cos(phase_angle).T, -weight[:, None] * jnp.sin(phase_angle).T],
        axis=0,
    ).astype(jnp.bfloat16)
    taper = 0.5 - 0.5 * jnp.cos(2.0 * math.pi / WINDOW * positions.astype(jnp.float32))
    return (forward, inverse, taper)


def fourier_table(length):
    positions = jnp.arange(length, dtype=jnp.int32)
    phase_angle = (
        2.0
        * math.pi
        / length
        * (positions[:, None] * positions[None, :] % length).astype(jnp.float32)
    )
    return (jnp.cos(phase_angle), jnp.sin(phase_angle))


def twist_table(first_index, second_index, length):
    product = first_index * second_index % length
    phase_angle = 2.0 * math.pi / length * product.astype(jnp.float32)
    return (jnp.cos(phase_angle), jnp.sin(phase_angle))


def apply_pair(pattern, cosine, sine_table, real_part, imag_part, direction):
    highest = lax.Precision.HIGHEST
    cos_real = jnp.einsum(pattern, cosine, real_part, precision=highest)
    cos_imag = jnp.einsum(pattern, cosine, imag_part, precision=highest)
    sin_real = jnp.einsum(pattern, sine_table, real_part, precision=highest)
    sin_imag = jnp.einsum(pattern, sine_table, imag_part, precision=highest)
    return (cos_real - direction * sin_imag, cos_imag + direction * sin_real)


def twist(real_part, imag_part, cosine, sine_table, direction):
    return (
        real_part * cosine - direction * imag_part * sine_table,
        imag_part * cosine + direction * real_part * sine_table,
    )


def on_device(signal, fan_mask):
    forward, inverse, taper = time_tables()
    position = lax.axis_index("tm")
    quarter = WINDOW // 4
    local_len = signal.shape[1]
    head_part = signal[:, :quarter]
    tail_part = signal[:, local_len - quarter :]
    outgoing = jnp.where(position == 0, tail_part, head_part)
    partner = partner_2(outgoing, "tm", 0)
    segment = jnp.where(
        position == 0,
        jnp.concatenate([signal, partner], axis=1),
        jnp.concatenate([partner, signal], axis=1),
    )
    tapered = (segment.astype(jnp.float32) * taper).astype(jnp.bfloat16)
    channel_rows = signal.shape[0]
    groups = lax.axis_size("chan")
    chan_pos = lax.axis_index("chan")
    total_channels = groups * channel_rows
    cosine_small, sine_small = fourier_table(groups)
    cosine_large, sine_large = fourier_table(channel_rows)
    offset_rows = channel_rows // groups
    spectrum = jnp.dot(tapered, forward, preferred_element_type=jnp.float32)
    pieces = spectrum.reshape(groups, offset_rows, 2, BAND)
    arrived = lax.all_to_all(pieces, "chan", split_axis=0, concat_axis=0, tiled=True)
    offsets = chan_pos * offset_rows + jnp.arange(offset_rows, dtype=jnp.int32)
    twist_cosine, twist_sine = twist_table(
        jnp.arange(groups, dtype=jnp.int32)[:, None], offsets[None, :], total_channels
    )
    twist_cosine = twist_cosine[:, :, None]
    twist_sine = twist_sine[:, :, None]
    real_part, imag_part = apply_pair(
        "ap,pjf->ajf", cosine_small, sine_small, arrived[:, :, 0], arrived[:, :, 1], -1.0
    )
    real_part, imag_part = twist(real_part, imag_part, twist_cosine, twist_sine, -1.0)
    turned = lax.all_to_all(
        jnp.stack([real_part, imag_part], axis=2), "chan", split_axis=0, concat_axis=1, tiled=True
    )
    lines = turned.reshape(channel_rows, 2, BAND)
    real_part, imag_part = apply_pair(
        "jb,jf->bf", cosine_large, sine_large, lines[:, 0], lines[:, 1], -1.0
    )
    expanded = (
        jnp.repeat(jnp.repeat(fan_mask, BIN_TILE, axis=0), WAVE_TILE // groups, axis=1)
        .astype(jnp.float32)
        .T
    )
    real_part = real_part * expanded
    imag_part = imag_part * expanded
    real_part, imag_part = apply_pair(
        "bj,bf->jf", cosine_large, sine_large, real_part, imag_part, 1.0
    )
    leaving = jnp.stack([real_part, imag_part], axis=1).reshape(1, channel_rows, 2, BAND)
    spread_back = lax.all_to_all(leaving, "chan", split_axis=1, concat_axis=0, tiled=True)
    real_part, imag_part = twist(
        spread_back[:, :, 0], spread_back[:, :, 1], twist_cosine, twist_sine, 1.0
    )
    real_part, imag_part = apply_pair(
        "pa,ajf->pjf", cosine_small, sine_small, real_part, imag_part, 1.0
    )
    result = jnp.stack([real_part, imag_part], axis=2) / total_channels
    returned = lax.all_to_all(
        result.astype(jnp.bfloat16), "chan", split_axis=0, concat_axis=0, tiled=True
    ).astype(result.dtype)
    parts = returned.astype(jnp.bfloat16).reshape(channel_rows, 2 * BAND)
    frame = jnp.dot(parts, inverse, preferred_element_type=jnp.float32) / WINDOW
    leaving_tail = jnp.where(position == 0, frame[:, 3 * quarter :], frame[:, :quarter])
    received = partner_2(leaving_tail.astype(jnp.bfloat16), "tm", 0).astype(leaving_tail.dtype)
    first_block = jnp.concatenate(
        [frame[:, : 2 * quarter], frame[:, 2 * quarter : 3 * quarter] + received], axis=1
    )
    second_block = jnp.concatenate(
        [frame[:, quarter : 2 * quarter] + received, frame[:, 2 * quarter :]], axis=1
    )
    return jnp.where(position == 0, first_block, second_block).astype(jnp.bfloat16)


def solution(mesh):
    placed = (P("chan", "tm"), P())
    return jax.shard_map(
        on_device, mesh=mesh, in_specs=placed, out_specs=P("chan", "tm"), check_vma=False
    )
```

profile of v0, /device:TPU:1, one launch (start us, length us, event | category | flops | bytes accessed | tf_op | source)
XLA Modules:
  0.0 199.1 jit_solution(4439925265711621370)
XLA Ops:
  0.0 1.1 slice_select_fusion.1
  1.1 2.1 %collective-permute-start = (bf16[128,1024]{1,0:T(8,128)(2,1)S(1)}, bf16[128,1024]{1,0:T(8,128)(2,1)S(1)}, u32[]{:S(2)}, u32[]{:S(2)}) collective-permute-start(bf16[128,1024]{1,0:T(8,128)(2,1)S(1)} %slice_select_fusion.1), channel_id=1, source_target_pairs={{0,1},{1,0},{2,3},{3,2},{4,5},{5,4},{6,7},{7,6},{8,9},{9,8},{10,11... | collective-permute-start | bytes 786440 | tf_op jit(solution)/shard_map/ppermute | solution.py:15
  3.2 33.9 %negate_convert_fusion = (bf16[4096,512]{1,0:T(8,128)(2,1)S(1)}, bf16[4096,512]{1,0:T(8,128)(2,1)S(1)}) fusion(), kind=kLoop, calls=%fused_computation.24 | loop fusion | flops 35651584 | bytes 8388608 | tf_op jit(solution)/shard_map/convert.3
  37.2 1.3 fusion.6
  38.5 1.2 reshape.211
  39.8 15.7 %all-to-all-start = ((f32[128,1,2,512]{3,2,1,0:T(2,128)}), f32[128,1,2,512]{3,2,1,0:T(2,128)S(1)}, u32[]{:S(2)}, u32[]{:S(2)}) async-start(f32[128,1,2,512]{3,2,1,0:T(2,128)} %bitcast), calls=%async_computation | async-start | bytes 1048576 | tf_op jit(solution)/shard_map/all_to_all | solution.py:92
  55.5 19.9 %all-to-all-done = f32[128,1,2,512]{3,2,1,0:T(2,128)S(1)} async-done(((f32[128,1,2,512]{3,2,1,0:T(2,128)}), f32[128,1,2,512]{3,2,1,0:T(2,128)S(1)}, u32[]{:S(2)}, u32[]{:S(2)}) %all-to-all-start) | async-done | bytes 524320 | tf_op jit(solution)/shard_map/all_to_all | solution.py:92
  77.8 0.7 subtract_bitcast_fusion
  78.6 1.2 copy.7
  79.8 6.8 %all-to-all-start.1 = ((f32[128,1,2,512]{3,2,1,0:T(2,128)}), f32[128,1,2,512]{3,2,1,0:T(2,128)S(1)}, u32[]{:S(2)}, u32[]{:S(2)}) async-start(f32[128,1,2,512]{3,2,1,0:T(2,128)} %copy.7), calls=%async_computation.1 | async-start | bytes 1048576 | tf_op jit(solution)/shard_map/all_to_all | solution.py:103
  86.8 19.8 %all-to-all-done.1 = f32[128,1,2,512]{3,2,1,0:T(2,128)S(1)} async-done(((f32[128,1,2,512]{3,2,1,0:T(2,128)}), f32[128,1,2,512]{3,2,1,0:T(2,128)S(1)}, u32[]{:S(2)}, u32[]{:S(2)}) %all-to-all-start.1) | async-done | bytes 524320 | tf_op jit(solution)/shard_map/all_to_all | solution.py:103
  112.4 1.2 copy.9
  113.6 6.8 %all-to-all-start.2 = ((f32[1,128,2,512]{3,2,0,1:T(2,128)}), f32[1,128,2,512]{3,2,0,1:T(2,128)S(1)}, u32[]{:S(2)}, u32[]{:S(2)}) async-start(f32[1,128,2,512]{3,2,0,1:T(2,128)} %copy.9), calls=%async_computation.2 | async-start | bytes 1048576 | tf_op jit(solution)/shard_map/all_to_all | solution.py:121
  120.5 19.9 %all-to-all-done.2 = f32[1,128,2,512]{3,2,0,1:T(2,128)S(1)} async-done(((f32[1,128,2,512]{3,2,0,1:T(2,128)}), f32[1,128,2,512]{3,2,0,1:T(2,128)S(1)}, u32[]{:S(2)}, u32[]{:S(2)}) %all-to-all-start.2) | async-done | bytes 524320 | tf_op jit(solution)/shard_map/all_to_all | solution.py:121
  140.5 0.7 fusion.73
  141.2 0.7 fusion.71
  141.9 0.7 fusion.25
  142.6 0.7 fusion.24
  143.4 1.0 copy.11
  144.3 6.8 %all-to-all-start.3 = ((bf16[128,1,2,512]{3,2,1,0:T(2,128)(2,1)}), bf16[128,1,2,512]{3,2,1,0:T(2,128)(2,1)S(1)}, u32[]{:S(2)}, u32[]{:S(2)}) async-start(bf16[128,1,2,512]{3,2,1,0:T(2,128)(2,1)} %copy.11), calls=%async_computation.3 | async-start | bytes 524288 | tf_op jit(solution)/shard_map/all_to_all | solution.py:129
  151.2 35.2 %multiply_convert_fusion = (bf16[512,4096]{1,0:T(8,128)(2,1)}, bf16[512,4096]{1,0:T(8,128)(2,1)}) fusion(f32[512]{0:T(512)S(1)} %fusion.92, f32[512]{0:T(512)S(1)} %fusion.91), kind=kLoop, calls=%fused_computation.20 | loop fusion | flops 37748736 | bytes 8392704 | tf_op jit(solution)/shard_map/convert.1
  186.6 4.2 %fusion.20 = f32[128,4096]{1,0:T(8,128)S(1)} fusion(bf16[128,1024]{0,1:T(8,128)(2,1)S(1)} %bitcast.77, bf16[512,4096]{1,0:T(8,128)(2,1)} %get-tuple-element.19, bf16[512,4096]{1,0:T(8,128)(2,1)} %get-tuple-element.20), kind=kOutput, calls=%fused_computation.30 | convolution fusion | flops 1091043328 | bytes 10747904 | tf_op jit(solution)/shard_map/dot_general | solution.py:133
  191.1 6.8 %collective-permute-done.1 = bf16[128,1024]{1,0:T(8,128)(2,1)S(1)} collective-permute-done((bf16[128,1024]{1,0:T(8,128)(2,1)S(1)}, bf16[128,1024]{1,0:T(8,128)(2,1)S(1)}, u32[]{:S(2)}, u32[]{:S(2)}) %collective-permute-start.1) | collective-permute-done | bytes 262176 | tf_op jit(solution)/shard_map/ppermute | solution.py:15
  198.0 1.1 fusion.23
  (36 shorter events, 9.3 us)
Async XLA Ops:
  1.1 36.2 %copy-start = (bf16[128,3072]{1,0:T(8,128)(2,1)S(1)}, bf16[128,3072]{1,0:T(8,128)(2,1)}, u32[]{:S(2)}) copy-start(bf16[128,3072]{1,0:T(8,128)(2,1)} %param.2) | copy-start | bytes 2359300
  1.1 36.1 %collective-permute-start = (bf16[128,1024]{1,0:T(8,128)(2,1)S(1)}, bf16[128,1024]{1,0:T(8,128)(2,1)S(1)}, u32[]{:S(2)}, u32[]{:S(2)}) collective-permute-start(bf16[128,1024]{1,0:T(8,128)(2,1)S(1)} %slice_select_fusion.1), channel_id=1, source_target_pairs={{0,1},{1,0},{2,3},{3,2},{4,5},{5,4},{6,7},{7,6},{8,9},{9,8},{10,11... | collective-permute-start | bytes 786440 | tf_op jit(solution)/shard_map/ppermute | solution.py:15
  39.8 46.9 %copy-start.1 = (s32[128,128]{1,0:T(8,128)S(1)}, s32[128,128]{1,0:T(8,128)}, u32[]{:S(2)}) copy-start(s32[128,128]{1,0:T(8,128)} %param.3) | copy-start | bytes 196612
  39.8 35.7 %all-to-all-start = ((f32[128,1,2,512]{3,2,1,0:T(2,128)}), f32[128,1,2,512]{3,2,1,0:T(2,128)S(1)}, u32[]{:S(2)}, u32[]{:S(2)}) async-start(f32[128,1,2,512]{3,2,1,0:T(2,128)} %bitcast), calls=%async_computation | async-start | bytes 1048576 | tf_op jit(solution)/shard_map/all_to_all | solution.py:92
  79.8 26.8 %all-to-all-start.1 = ((f32[128,1,2,512]{3,2,1,0:T(2,128)}), f32[128,1,2,512]{3,2,1,0:T(2,128)S(1)}, u32[]{:S(2)}, u32[]{:S(2)}) async-start(f32[128,1,2,512]{3,2,1,0:T(2,128)} %copy.7), calls=%async_computation.1 | async-start | bytes 1048576 | tf_op jit(solution)/shard_map/all_to_all | solution.py:103
  113.6 26.8 %all-to-all-start.2 = ((f32[1,128,2,512]{3,2,0,1:T(2,128)}), f32[1,128,2,512]{3,2,0,1:T(2,128)S(1)}, u32[]{:S(2)}, u32[]{:S(2)}) async-start(f32[1,128,2,512]{3,2,0,1:T(2,128)} %copy.9), calls=%async_computation.2 | async-start | bytes 1048576 | tf_op jit(solution)/shard_map/all_to_all | solution.py:121
  144.3 42.0 %all-to-all-start.3 = ((bf16[128,1,2,512]{3,2,1,0:T(2,128)(2,1)}), bf16[128,1,2,512]{3,2,1,0:T(2,128)(2,1)S(1)}, u32[]{:S(2)}, u32[]{:S(2)}) async-start(bf16[128,1,2,512]{3,2,1,0:T(2,128)(2,1)} %copy.11), calls=%async_computation.3 | async-start | bytes 524288 | tf_op jit(solution)/shard_map/all_to_all | solution.py:129
  190.9 7.0 %collective-permute-start.1 = (bf16[128,1024]{1,0:T(8,128)(2,1)S(1)}, bf16[128,1024]{1,0:T(8,128)(2,1)S(1)}, u32[]{:S(2)}, u32[]{:S(2)}) collective-permute-start(bf16[128,1024]{1,0:T(8,128)(2,1)S(1)} %fusion.41), channel_id=1, source_target_pairs={{0,1},{1,0},{2,3},{3,2},{4,5},{5,4},{6,7},{7,6},{8,9},{9,8},{10,11... | collective-permute-start | bytes 786440 | tf_op jit(solution)/shard_map/ppermute | solution.py:15
where the time goes:
time: 200 us; the launch traced here: 199 us
  other arithmetic  71.7 us (36%)
  waiting for transfers between devices  66.3 us (33%)
  starting transfers between devices  38.4 us (19%)
  matrix products  16.3 us (8%)
  local copies, waits for them, and re-layouts  6.07 us (3%)
    another operation x2, other arithmetic  69.1 us
    all_to_all x1, waiting for transfers between devices, on_device(): lax.all_to_all(pieces, 'chan', split_axis=0, concat_axis=0, tiled=True)  19.9 us
    all_to_all x1, waiting for transfers between devices, on_device(): lax.all_to_all(leaving, 'chan', split_axis=1, concat_axis=0, tiled=True)  19.9 us
    all_to_all x1, waiting for transfers between devices, on_device(): lax.all_to_all(jnp.stack([real_part, imag_part], axis=2), 'chan', split_a...  19.8 us
    all_to_all x1, starting transfers between devices, on_device(): lax.all_to_all(pieces, 'chan', split_axis=0, concat_axis=0, tiled=True)  15.7 us
    all_to_all x1, starting transfers between devices, on_device(): lax.all_to_all(jnp.stack([real_part, imag_part], axis=2), 'chan', split_a...  6.84 us
    all_to_all x1, starting transfers between devices, on_device(): lax.all_to_all(result.astype(jnp.bfloat16), 'chan', split_axis=0, concat_...  6.84 us
    all_to_all x1, starting transfers between devices, on_device(): lax.all_to_all(leaving, 'chan', split_axis=1, concat_axis=0, tiled=True)  6.83 us
  transfers between devices with their start and end apart: 6, of which 4 were waited for; matrix products, arithmetic and copies ran while one was open for 35% of the time, Pallas kernels for 0%

commit v1 on v0

v1 whole, which is shorter than its diff:
```python
import functools
import math

import jax
import jax.numpy as jnp
import ml_dtypes
import numpy as np
from jax import lax
from jax.experimental import pallas as pl
from jax.experimental.pallas import tpu as pltpu
from jax.sharding import PartitionSpec as P

WINDOW = 4096
BAND = 512
QUARTER = WINDOW // 4
LINES = 128
BINS = 4
ROWS = 2 * BINS
MESH = pl.DeviceIdType.MESH
F32 = jnp.float32
BF16 = jnp.bfloat16


def high_low(table):
    high = table.astype(ml_dtypes.bfloat16)
    low = (table - high.astype(np.float64)).astype(ml_dtypes.bfloat16)
    return high, low


@functools.cache
def tables():
    positions = np.arange(WINDOW)
    bins = np.arange(BAND)
    angle = 2.0 * math.pi / WINDOW * (positions[:, None] * bins[None, :] % WINDOW)
    cosine, sine = np.cos(angle), np.sin(angle)
    forward = np.stack([cosine, -sine], axis=1).reshape(WINDOW, 2, LINES, BINS)
    forward = forward.transpose(0, 2, 1, 3).reshape(4, QUARTER, 2 * BAND)
    weight = np.where(bins == 0, 1.0, 2.0)
    inverse = np.stack([weight * cosine, -weight * sine], axis=1).reshape(WINDOW, 2, LINES, BINS)
    inverse = inverse.transpose(2, 1, 3, 0).reshape(2 * BAND, 4, QUARTER).transpose(1, 0, 2)
    taper = (0.5 - 0.5 * np.cos(2.0 * math.pi / WINDOW * positions)).reshape(1, WINDOW)
    lines = np.arange(LINES)
    angle = 2.0 * math.pi / LINES * (lines[:, None] * lines[None, :] % LINES)
    cosine, sine = np.cos(angle), np.sin(angle)
    analysis = np.block([[cosine, sine], [-sine, cosine]])
    synthesis = np.block([[cosine, -sine], [sine, cosine]]) / LINES
    turns = np.stack(high_low(analysis) + high_low(synthesis))
    angle = 2.0 * math.pi / LINES**2 * (lines[:, None] * lines[None, :])
    fine = np.stack([np.cos(angle), np.sin(angle), cosine, sine]).astype(np.float32)
    return (
        forward.astype(ml_dtypes.bfloat16),
        inverse.astype(ml_dtypes.bfloat16),
        taper.astype(np.float32),
        turns,
        fine,
    )


def hops(step):
    core, z, y, x = step
    return min(z, 8 - z) + min(y, 4 - y) + 2 * x + 0.25 * core


def kernel(
    signal, mask, forward, inverse, taper, turns, fine, out,
    sig, mask_v, fwd, inv, taper_v, turns_v, fine_v, near, acc, send1, got1, send2, got2,
    lines_v, back_v, leaving, received,
    local, table_sem, link_send, link_recv,
):
    me, tm = lax.axis_index("chan"), lax.axis_index("tm")
    rem, div = lax.rem, lax.div
    core, z, y, x = rem(me, 2), rem(div(me, 2), 8), rem(div(me, 16), 4), div(me, 64)
    steps = [(c, k, j, i) for i in range(2) for j in range(4) for k in range(8) for c in range(2)]
    steps = sorted(steps[1:], key=hops, reverse=True)

    def device(step):
        c, k, j, i = step
        return ((rem(x + i, 2) * 4 + rem(y + j, 4)) * 8 + rem(z + k, 8)) * 2 + rem(core + c, 2)

    barrier = pltpu.get_barrier_semaphore()
    pl.semaphore_signal(barrier, 1, device_id={"tm": 1 - tm}, device_id_type=MESH)
    for step in steps:
        pl.semaphore_signal(barrier, 1, device_id={"chan": device(step)}, device_id_type=MESH)

    own = [tm + i for i in range(3)]
    other = 3 * (1 - tm)
    small = [(signal, sig), (taper, taper_v), (mask, mask_v), (fine, fine_v), (turns, turns_v)]
    small = [pltpu.make_async_copy(a, b, local.at[i]) for i, (a, b) in enumerate(small)]
    order = own + [other]
    fwd_copies = [pltpu.make_async_copy(forward.at[q], fwd.at[q], table_sem.at[i]) for i, q in enumerate(order)]
    inv_copies = [pltpu.make_async_copy(inverse.at[q], inv.at[q], table_sem.at[4 + q]) for q in range(4)]
    for copy in small + fwd_copies + inv_copies:
        copy.start()

    small[0].wait()
    pl.semaphore_wait(barrier, LINES)
    edge = pl.multiple_of((1 - tm) * 2 * QUARTER, QUARTER)
    swap = pltpu.make_async_remote_copy(
        sig.at[:, pl.ds(edge, QUARTER)], near, link_send.at[0], link_recv.at[0],
        device_id={"tm": 1 - tm}, device_id_type=MESH,
    )
    swap.start()

    for copy in small[1:]:
        copy.wait()
    passes = mask_v[pl.ds(me, 1), :].astype(F32) * (1.0 / LINES)
    cosine, sine = fine_v[2], fine_v[3]
    highest = lax.Precision.HIGHEST
    left = jnp.concatenate([cosine * passes, sine * passes], axis=1)
    right = jnp.concatenate(
        [jnp.concatenate([cosine, sine], axis=1), jnp.concatenate([sine, -cosine], axis=1)], axis=0
    )
    fan = jnp.dot(left, right, precision=highest, preferred_element_type=F32)
    fan = jnp.concatenate(
        [fan, jnp.concatenate([-fan[:, LINES:], fan[:, :LINES]], axis=1)], axis=0
    )
    fan_high = fan.astype(BF16)
    fan_low = (fan - fan_high.astype(F32)).astype(BF16)

    def part(samples, quarter):
        weights = taper_v[:, pl.ds(pl.multiple_of(quarter * QUARTER, QUARTER), QUARTER)]
        tapered = (samples.astype(F32) * weights).astype(BF16)
        return jnp.dot(tapered, fwd[quarter], preferred_element_type=F32)

    for i in range(3):
        fwd_copies[i].wait()
        term = part(sig[:, i * QUARTER : (i + 1) * QUARTER], own[i])
        if i == 0:
            acc[...] = term
        else:
            acc[...] += term
    fwd_copies[3].wait()
    swap.wait_recv()
    spectrum = acc[...] + part(near[...], other)
    send1[...] = spectrum.T.reshape(LINES, ROWS, LINES).astype(BF16)

    def exchange(source, target, slot):
        for step in steps:
            d = device(step)
            pltpu.make_async_remote_copy(
                source.at[d], target.at[me], link_send.at[slot], link_recv.at[slot],
                device_id={"chan": d}, device_id_type=MESH,
            ).start()
        target[me] = source[me]
        rest = pl.ds(0, LINES - 1)
        return pltpu.make_async_remote_copy(
            source.at[rest], target.at[rest], link_send.at[slot], link_recv.at[slot],
            device_id={"chan": device(steps[0])}, device_id_type=MESH,
        )

    first = exchange(send1, got1, 1)
    first.wait_recv()
    lines_v[...] = got1[...].astype(F32).reshape(ROWS * LINES, LINES)
    picked = [lines_v[pl.ds(r, LINES, stride=ROWS), :].astype(BF16) for r in range(ROWS)]
    stacked = jnp.concatenate(
        [jnp.concatenate(picked[:BINS], axis=1), jnp.concatenate(picked[BINS:], axis=1)], axis=0
    )
    wave = jnp.dot(turns_v[0], stacked, preferred_element_type=F32)
    wave += jnp.dot(turns_v[1], stacked, preferred_element_type=F32)
    twist_cos, twist_sin = fine_v[0], fine_v[1]
    turned = []
    for j in range(BINS):
        re = wave[:LINES, j * LINES : (j + 1) * LINES]
        im = wave[LINES:, j * LINES : (j + 1) * LINES]
        turned.append(
            jnp.concatenate(
                [re * twist_cos + im * twist_sin, im * twist_cos - re * twist_sin], axis=1
            )
        )
    turned = jnp.concatenate(turned, axis=0)
    high = turned.astype(BF16)
    low = (turned - high.astype(F32)).astype(BF16)
    masked = jnp.dot(high, fan_high, preferred_element_type=F32)
    masked += jnp.dot(low, fan_high, preferred_element_type=F32)
    masked += jnp.dot(high, fan_low, preferred_element_type=F32)
    real, imag = [], []
    for j in range(BINS):
        re = masked[j * LINES : (j + 1) * LINES, :LINES]
        im = masked[j * LINES : (j + 1) * LINES, LINES:]
        real.append(re * twist_cos - im * twist_sin)
        imag.append(im * twist_cos + re * twist_sin)
    straight = jnp.concatenate(
        [jnp.concatenate(real, axis=1), jnp.concatenate(imag, axis=1)], axis=0
    )
    high = straight.astype(BF16)
    low = (straight - high.astype(F32)).astype(BF16)
    back = jnp.dot(turns_v[2], high, preferred_element_type=F32)
    back += jnp.dot(turns_v[2], low, preferred_element_type=F32)
    back += jnp.dot(turns_v[3], high, preferred_element_type=F32)
    for r in range(ROWS):
        top, column = r // BINS * LINES, r % BINS * LINES
        lines_v[pl.ds(r, LINES, stride=ROWS), :] = back[top : top + LINES, column : column + LINES]
    send2[...] = lines_v[...].reshape(LINES, ROWS, LINES).astype(BF16)
    second = exchange(send2, got2, 2)
    for copy in inv_copies:
        copy.wait()
    second.wait_recv()
    back_v[...] = got2[...].astype(F32).reshape(ROWS * LINES, LINES).T.astype(BF16)

    def frame(quarter):
        return jnp.dot(back_v[...], inv[quarter], preferred_element_type=F32) * (1.0 / WINDOW)

    leaving[...] = frame(other).astype(BF16)
    tail = pltpu.make_async_remote_copy(
        leaving, received, link_send.at[3], link_recv.at[3],
        device_id={"tm": 1 - tm}, device_id_type=MESH,
    )
    tail.start()
    outer = pl.multiple_of(2 * QUARTER * tm, QUARTER)
    shared = pl.multiple_of(2 * QUARTER * (1 - tm), QUARTER)
    out[:, pl.ds(outer, QUARTER)] = frame(3 * tm).astype(BF16)
    out[:, QUARTER : 2 * QUARTER] = frame(1 + tm).astype(BF16)
    acc[...] = frame(2 - tm)
    tail.wait_recv()
    out[:, pl.ds(shared, QUARTER)] = (acc[...] + received[...].astype(F32)).astype(BF16)
    swap.wait_send()
    first.wait_send()
    second.wait_send()
    tail.wait_send()


def on_device(signal, fan_mask):
    anywhere = pl.BlockSpec(memory_space=pl.ANY)
    block = (LINES, ROWS, LINES)
    dma = pltpu.SemaphoreType.DMA
    vmem = pltpu.VMEM
    return pl.pallas_call(
        kernel,
        out_shape=jax.ShapeDtypeStruct(signal.shape, BF16),
        in_specs=[anywhere] * 7,
        out_specs=pl.BlockSpec(memory_space=pltpu.VMEM),
        scratch_shapes=[
            vmem(signal.shape, BF16),
            vmem((LINES, LINES), jnp.int32),
            vmem((4, QUARTER, 2 * BAND), BF16),
            vmem((4, 2 * BAND, QUARTER), BF16),
            vmem((1, WINDOW), F32),
            vmem((4, 2 * LINES, 2 * LINES), BF16),
            vmem((4, LINES, LINES), F32),
            vmem((LINES, QUARTER), BF16),
            vmem((LINES, 2 * BAND), F32),
            vmem(block, BF16),
            vmem(block, BF16),
            vmem(block, BF16),
            vmem(block, BF16),
            vmem((ROWS * LINES, LINES), F32),
            vmem((LINES, 2 * BAND), BF16),
            vmem((LINES, QUARTER), BF16),
            vmem((LINES, QUARTER), BF16),
            dma((5,)),
            dma((8,)),
            dma((4,)),
            dma((4,)),
        ],
        compiler_params=pltpu.CompilerParams(
            collective_id=0, has_side_effects=True, vmem_limit_bytes=48 * 2**20
        ),
        cost_estimate=pl.CostEstimate(
            flops=5 * 10**9, bytes_accessed=20 * 10**6, transcendentals=0
        ),
    )(signal, fan_mask, *tables())


def solution(mesh):
    return jax.shard_map(
        on_device,
        mesh=mesh,
        in_specs=(P("chan", "tm"), P()),
        out_specs=P("chan", "tm"),
        check_vma=False,
    )
```

time: 200 us -> 53.7 us (0.27)
  other arithmetic: 71.7 us -> 0 us
  waiting for transfers between devices: 66.3 us -> 0 us
  Pallas kernels: 0 us -> 47.9 us
  starting transfers between devices: 38.4 us -> 0 us
  matrix products: 16.3 us -> 0 us
    another operation x3 -> x0, other arithmetic: 69.1 us -> none
    all_to_all x4 -> x0, waiting for transfers between devices: 59.6 us -> none  [the longest x1 19.9 us: on_device(): lax.all_to_all(pieces, 'chan', split_axis=0, concat_axis=0, tiled=True)]
    pallas_call x0 -> x1, Pallas kernels: none -> 47.9 us  [on_device(): pl.pallas_call(kernel, out_shape=jax.ShapeDtypeStruct(signal.shape, BF16)...]
    all_to_all x4 -> x0, starting transfers between devices: 36.2 us -> none  [the longest x1 15.7 us: on_device(): lax.all_to_all(pieces, 'chan', split_axis=0, concat_axis=0, tiled=True)]
    dot_general x18 -> x0, matrix products: 16.3 us -> none  [the longest x1 4.25 us: on_device(): frame = jnp.dot(parts, inverse, preferred_element_type=jnp.float32) / WINDOW]
    ppermute x2 -> x0, waiting for transfers between devices: 6.76 us -> none  [partner_2(): lax.ppermute(array, axis, [(i, i ^ 1 << distance) for i in range(lax.axis...]
    unnamed x4 -> x11, local copies, waits for them, and re-layouts: 0.01 us -> 5.56 us
    reshape x2 -> x0, local copies, waits for them, and re-layouts: 2.43 us -> none  [the longest x1 1.23 us: on_device(): pieces = spectrum.reshape(groups, offset_rows, 2, BAND)]
  transfers between devices with their start and end apart: 6 -> 0, of which waited for: 4 -> 0; matrix products, arithmetic and copies ran while one was open for 35% -> 0% of each run, Pallas kernels for 0% -> 0%
where the time goes in v1:
time: 53.7 us; the launch traced here: 53.4 us
  Pallas kernels  47.9 us (89%)
  local copies, waits for them, and re-layouts  5.56 us (10%)
    pallas_call x1, Pallas kernels, on_device(): pl.pallas_call(kernel, out_shape=jax.ShapeDtypeStruct(signal.shape, BF16)...  47.9 us
    unnamed x11, local copies, waits for them, and re-layouts  5.56 us

profile of v1, /device:TPU:1, one launch (start us, length us, event | category | flops | bytes accessed | tf_op | source)
XLA Modules:
  0.0 53.4 jit_solution(11723208000145208182)
XLA Ops:
  0.0 0.0 copy-start
  0.0 1.1 %copy-done = bf16[128,3072]{1,0:T(8,128)(2,1)S(1)} copy-done((bf16[128,3072]{1,0:T(8,128)(2,1)S(1)}, bf16[128,3072]{1,0:T(8,128)(2,1)}, u32[]{:S(2)}) %copy-start) | copy-done | bytes 786456
  1.1 0.0 copy-start.1
  1.1 1.0 %copy-done.1 = bf16[4,256,256]{2,1,0:T(8,128)(2,1)S(1)} copy-done((bf16[4,256,256]{2,1,0:T(8,128)(2,1)S(1)}, bf16[4,256,256]{2,1,0:T(8,128)(2,1)}, u32[]{:S(2)}) %copy-start.1) | copy-done | bytes 524312
  2.2 0.0 copy-start.2
  2.2 0.9 %copy-done.2 = f32[4,128,128]{2,1,0:T(8,128)S(1)} copy-done((f32[4,128,128]{2,1,0:T(8,128)S(1)}, f32[4,128,128]{2,1,0:T(8,128)}, u32[]{:S(2)}) %copy-start.2) | copy-done | bytes 262168
  3.1 0.0 copy-start.3
  3.1 0.8 %copy-done.3 = s32[128,128]{1,0:T(8,128)S(1)} copy-done((s32[128,128]{1,0:T(8,128)S(1)}, s32[128,128]{1,0:T(8,128)}, u32[]{:S(2)}) %copy-start.3) | copy-done | bytes 65560
  4.0 0.0 copy-start.4
  4.0 0.7 %copy-done.4 = f32[1,4096]{1,0:T(1,128)S(1)} copy-done((f32[1,4096]{1,0:T(1,128)S(1)}, f32[1,4096]{1,0:T(1,128)}, u32[]{:S(2)}) %copy-start.4) | copy-done | bytes 16408
  4.7 47.9 %shard_map.73 = bf16[128,3072]{1,0:T(8,128)(2,1)S(1)} custom-call(bf16[128,3072]{1,0:T(8,128)(2,1)S(1)} %copy-done, s32[128,128]{1,0:T(8,128)S(1)} %copy-done.3, bf16[4,1024,1024]{2,1,0:T(8,128)(2,1)} %constant.10.clone.forward, bf16[4,1024,1024]{2,1,0:T(8,128)(2,1)} %constant.11.clone.inverse, f32[1,4096]{1,0:T(1,128)S(1)} %copy-done.4, ...), custom_call_target="tpu_custom_call" | custom-call | flops 5000000000 | bytes 20000000 | tf_op jit(solution)/shard_map/pallas_call | solution.py:227
  52.5 0.9 %copy.9 = bf16[128,3072]{1,0:T(8,128)(2,1)} copy(bf16[128,3072]{1,0:T(8,128)(2,1)S(1)} %shard_map.73) | data formatting | bytes 1572864
Async XLA Ops:
  0.0 1.1 %copy-start = (bf16[128,3072]{1,0:T(8,128)(2,1)S(1)}, bf16[128,3072]{1,0:T(8,128)(2,1)}, u32[]{:S(2)}) copy-start(bf16[128,3072]{1,0:T(8,128)(2,1)} %signal.1) | copy-start | bytes 2359300
  1.1 1.0 %copy-start.1 = (bf16[4,256,256]{2,1,0:T(8,128)(2,1)S(1)}, bf16[4,256,256]{2,1,0:T(8,128)(2,1)}, u32[]{:S(2)}) copy-start(bf16[4,256,256]{2,1,0:T(8,128)(2,1)} %constant.13.clone.turns) | copy-start | bytes 1572868
  2.2 0.9 %copy-start.2 = (f32[4,128,128]{2,1,0:T(8,128)S(1)}, f32[4,128,128]{2,1,0:T(8,128)}, u32[]{:S(2)}) copy-start(f32[4,128,128]{2,1,0:T(8,128)} %constant.14.clone.fine) | copy-start | bytes 786436
  3.1 0.8 %copy-start.3 = (s32[128,128]{1,0:T(8,128)S(1)}, s32[128,128]{1,0:T(8,128)}, u32[]{:S(2)}) copy-start(s32[128,128]{1,0:T(8,128)} %mask.1) | copy-start | bytes 196612
  4.0 0.7 %copy-start.4 = (f32[1,4096]{1,0:T(1,128)S(1)}, f32[1,4096]{1,0:T(1,128)}, u32[]{:S(2)}) copy-start(f32[1,4096]{1,0:T(1,128)} %constant.12.clone.taper) | copy-start | bytes 49156

commit v2 on v1

v2 whole, which is shorter than its diff:
```python
import functools
import math

import jax
import jax.numpy as jnp
import ml_dtypes
import numpy as np
from jax import lax
from jax.experimental import pallas as pl
from jax.experimental.pallas import tpu as pltpu
from jax.sharding import PartitionSpec as P

WINDOW = 4096
BAND = 512
QUARTER = WINDOW // 4
LINES = 128
BINS = 4
ROWS = 2 * BINS
MESH = pl.DeviceIdType.MESH
F32 = jnp.float32
BF16 = jnp.bfloat16


def high_low(table):
    high = table.astype(ml_dtypes.bfloat16)
    low = (table - high.astype(np.float64)).astype(ml_dtypes.bfloat16)
    return high, low


@functools.cache
def tables():
    positions = np.arange(WINDOW)
    bins = np.arange(BAND)
    angle = 2.0 * math.pi / WINDOW * (positions[:, None] * bins[None, :] % WINDOW)
    cosine, sine = np.cos(angle), np.sin(angle)
    places = np.arange(LINES).reshape(2, 4, 8, 2).transpose(2, 0, 1, 3).reshape(LINES)
    forward = np.stack([cosine, -sine], axis=1).reshape(WINDOW, 2, LINES, BINS)[:, :, places]
    forward = forward.transpose(0, 2, 1, 3).reshape(4, QUARTER, 2 * BAND)
    weight = np.where(bins == 0, 1.0, 2.0)
    inverse = np.stack([weight * cosine, -weight * sine], axis=1)
    inverse = inverse.reshape(WINDOW, 2, LINES, BINS)[:, :, places]
    inverse = inverse.transpose(2, 1, 3, 0).reshape(2 * BAND, 4, QUARTER).transpose(1, 0, 2)
    taper = (0.5 - 0.5 * np.cos(2.0 * math.pi / WINDOW * positions)).reshape(1, WINDOW)
    lines = np.arange(LINES)
    angle = 2.0 * math.pi / LINES * (lines[:, None] * lines[None, :] % LINES)
    cosine, sine = np.cos(angle), np.sin(angle)
    analysis = np.block([[cosine, sine], [-sine, cosine]])[:, np.r_[places, LINES + places]]
    synthesis = np.block([[cosine, -sine], [sine, cosine]])[np.r_[places, LINES + places]] / LINES
    turns = np.stack(high_low(analysis) + high_low(synthesis))
    angle = 2.0 * math.pi / LINES**2 * (lines[:, None] * lines[None, :])
    fine = np.stack([np.cos(angle), np.sin(angle), cosine, sine]).astype(np.float32)
    return (
        forward.astype(ml_dtypes.bfloat16),
        inverse.astype(ml_dtypes.bfloat16),
        taper.astype(np.float32),
        turns,
        fine,
    )


def hops(step):
    x, y, core = step
    return 2 * x + min(y, 4 - y) + 0.25 * core


LAYERS = 8
AROUND = LINES // LAYERS
Z_STEPS = (4, 3, 5, 2, 6, 1, 7, 0)
PLANE_STEPS = sorted(((i, j, c) for i in range(2) for j in range(4) for c in range(2)), key=hops, reverse=True)


def kernel(
    signal, mask, forward, inverse, taper, turns, fine, out,
    sig, mask_v, fwd, inv, taper_v, turns_v, fine_v, own_part, other_part, arrived_part,
    send1, got1, send2, got2, passed, lines_v, back_v, other_v,
    local, table_sem, swap_send, swap_recv, send_sem, recv1, recv2, pass_send, pass_recv,
):
    me, tm = lax.axis_index("chan"), lax.axis_index("tm")
    rem, div = lax.rem, lax.div
    core, z, y, x = rem(me, 2), rem(div(me, 2), 8), rem(div(me, 16), 4), div(me, 64)
    layers = [rem(z + k, LAYERS) for k in Z_STEPS]
    plane = [(rem(x + i, 2), rem(y + j, 4), rem(core + c, 2)) for i, j, c in PLANE_STEPS]
    here = z * AROUND + (x * 4 + y) * 2 + core
    partner = {"tm": 1 - tm}

    def peers(layer, first):
        for i, j, c in plane[: AROUND - first]:
            yield layer * AROUND + (i * 4 + j) * 2 + c, ((i * 4 + j) * 8 + layer) * 2 + c

    everyone = [(k, peers(layer, Z_STEPS[k] == 0)) for k, layer in enumerate(layers)]
    everyone = [list(p) for _, p in everyone]

    barrier = pltpu.get_barrier_semaphore()
    pl.semaphore_signal(barrier, 1, device_id=partner, device_id_type=MESH)
    for group in everyone:
        for _, d in group:
            pl.semaphore_signal(barrier, 1, device_id={"chan": d}, device_id_type=MESH)

    small = [(signal, sig), (taper, taper_v), (mask, mask_v), (fine, fine_v), (turns, turns_v)]
    small = [pltpu.make_async_copy(a, b, local.at[i]) for i, (a, b) in enumerate(small)]
    edge = 3 * tm
    quarters = [edge, 1, 2]
    fwd_copies = [pltpu.make_async_copy(forward.at[q], fwd.at[i], table_sem.at[i]) for i, q in enumerate(quarters)]
    inv_copies = [pltpu.make_async_copy(inverse.at[q], inv.at[i], table_sem.at[3 + i]) for i, q in enumerate(quarters)]
    for copy in small + fwd_copies + inv_copies:
        copy.start()

    outer = pl.multiple_of(2 * QUARTER * tm, QUARTER)
    shared = pl.multiple_of(2 * QUARTER * (1 - tm), QUARTER)

    def tapered(offset, quarter):
        weights = taper_v[:, pl.ds(pl.multiple_of(quarter * QUARTER, QUARTER), QUARTER)]
        return (sig[:, pl.ds(offset, QUARTER)].astype(F32) * weights).astype(BF16)

    small[0].wait()
    small[1].wait()
    both = jnp.concatenate([tapered(shared, edge), tapered(outer, edge)], axis=0)
    fwd_copies[0].wait()
    both = jnp.dot(both, fwd[0], preferred_element_type=F32)
    other_part[...] = both[:LINES].T.reshape(LAYERS, LINES, LINES).astype(BF16)
    pl.semaphore_wait(barrier, LINES)
    swaps = []
    for k, layer in enumerate(layers):
        swaps.append(
            pltpu.make_async_remote_copy(
                other_part.at[layer], arrived_part.at[layer], swap_send.at[k], swap_recv.at[k],
                device_id=partner, device_id_type=MESH,
            )
        )
        swaps[-1].start()
    middle = [pl.multiple_of(QUARTER * (1 - tm), QUARTER), pl.multiple_of(QUARTER * (2 - tm), QUARTER)]
    total = both[LINES:]
    for i in range(2):
        fwd_copies[1 + i].wait()
        total += jnp.dot(tapered(middle[i], 1 + i), fwd[1 + i], preferred_element_type=F32)
    own_part[...] = total.T.reshape(LAYERS, LINES, LINES)

    def start(source, target, place, d, send, recv):
        pltpu.make_async_remote_copy(
            source.at[place], target.at[here], send, recv, device_id={"chan": d}, device_id_type=MESH
        ).start()

    for k, layer in enumerate(layers):
        swaps[k].wait_recv()
        lines = own_part[layer] + arrived_part[layer].astype(F32)
        send1[pl.ds(layer * AROUND, AROUND)] = lines.reshape(AROUND, ROWS, LINES).astype(BF16)
        for place, d in everyone[k]:
            start(send1, got1, place, d, send_sem.at[0], recv1)
    got1[here] = send1[here]

    for copy in small[2:]:
        copy.wait()
    passes = mask_v[pl.ds(me, 1), :].astype(F32) * (1.0 / LINES)
    cosine, sine = fine_v[2], fine_v[3]
    left = jnp.concatenate([cosine * passes, sine * passes], axis=1)
    right = jnp.concatenate(
        [jnp.concatenate([cosine, sine], axis=1), jnp.concatenate([sine, -cosine], axis=1)], axis=0
    )
    fan = jnp.dot(left, right, precision=lax.Precision.HIGHEST, preferred_element_type=F32)
    fan = jnp.concatenate(
        [fan, jnp.concatenate([-fan[:, LINES:], fan[:, :LINES]], axis=1)], axis=0
    )
    fan_high = fan.astype(BF16)
    fan_low = (fan - fan_high.astype(F32)).astype(BF16)

    def whole(source, target, send, recv):
        rest = pl.ds(0, LINES - 1)
        return pltpu.make_async_remote_copy(
            source.at[rest], target.at[rest], send, recv,
            device_id={"chan": everyone[0][0][1]}, device_id_type=MESH,
        )

    first = whole(send1, got1, send_sem.at[0], recv1)
    first.wait_recv()
    lines_v[...] = got1[...].astype(F32).reshape(ROWS * LINES, LINES)
    picked = [lines_v[pl.ds(r, LINES, stride=ROWS), :].astype(BF16) for r in range(ROWS)]
    stacked = jnp.concatenate(
        [jnp.concatenate(picked[:BINS], axis=1), jnp.concatenate(picked[BINS:], axis=1)], axis=0
    )
    wave = jnp.dot(turns_v[0], stacked, preferred_element_type=F32)
    wave += jnp.dot(turns_v[1], stacked, preferred_element_type=F32)
    twist_cos, twist_sin = fine_v[0], fine_v[1]
    turned = []
    for j in range(BINS):
        re = wave[:LINES, j * LINES : (j + 1) * LINES]
        im = wave[LINES:, j * LINES : (j + 1) * LINES]
        turned.append(
            jnp.concatenate(
                [re * twist_cos + im * twist_sin, im * twist_cos - re * twist_sin], axis=1
            )
        )
    turned = jnp.concatenate(turned, axis=0)
    high = turned.astype(BF16)
    low = (turned - high.astype(F32)).astype(BF16)
    masked = jnp.dot(high, fan_high, preferred_element_type=F32)
    masked += jnp.dot(low, fan_high, preferred_element_type=F32)
    masked += jnp.dot(high, fan_low, preferred_element_type=F32)
    real, imag = [], []
    for j in range(BINS):
        re = masked[j * LINES : (j + 1) * LINES, :LINES]
        im = masked[j * LINES : (j + 1) * LINES, LINES:]
        real.append(re * twist_cos - im * twist_sin)
        imag.append(im * twist_cos + re * twist_sin)
    straight = jnp.concatenate(
        [jnp.concatenate(real, axis=1), jnp.concatenate(imag, axis=1)], axis=0
    )
    high = straight.astype(BF16)
    low = (straight - high.astype(F32)).astype(BF16)
    back = jnp.dot(turns_v[2], high, preferred_element_type=F32)
    back += jnp.dot(turns_v[2], low, preferred_element_type=F32)
    back += jnp.dot(turns_v[3], high, preferred_element_type=F32)
    for r in range(ROWS):
        top, column = r // BINS * LINES, r % BINS * LINES
        lines_v[pl.ds(r, LINES, stride=ROWS), :] = back[top : top + LINES, column : column + LINES]
    send2[...] = lines_v[...].reshape(LINES, ROWS, LINES).astype(BF16)
    for group in everyone:
        for place, d in group:
            start(send2, got2, place, d, send_sem.at[1], recv2.at[z])
    got2[here] = send2[here]

    def turn(source, target, layer):
        block = source[pl.ds(layer * AROUND, AROUND)].astype(F32).reshape(LINES, LINES)
        target[:, pl.ds(pl.multiple_of(layer * LINES, LINES), LINES)] = block.T.astype(BF16)

    passing = []
    for k, layer in enumerate(layers):
        count = pl.ds(0, len(everyone[k]))
        pltpu.make_async_remote_copy(
            send2.at[count], got2.at[count], send_sem.at[1], recv2.at[layer],
            device_id=partner, device_id_type=MESH,
        ).wait_recv()
        block = pl.ds(layer * AROUND, AROUND)
        passing.append(
            pltpu.make_async_remote_copy(
                got2.at[block], passed.at[block], pass_send.at[k], pass_recv.at[k],
                device_id=partner, device_id_type=MESH,
            )
        )
        passing[-1].start()
        turn(got2, back_v, layer)

    def frame(values, i):
        return jnp.dot(values, inv[i], preferred_element_type=F32) * (1.0 / WINDOW)

    for copy in inv_copies:
        copy.wait()
    out[:, pl.ds(outer, QUARTER)] = frame(back_v[...], 0).astype(BF16)
    centre = 1 + tm
    out[:, QUARTER : 2 * QUARTER] = frame(back_v[...], centre).astype(BF16)
    overlap = frame(back_v[...], 2 - tm)
    for k, layer in enumerate(layers):
        passing[k].wait_recv()
        turn(passed, other_v, layer)
    out[:, pl.ds(shared, QUARTER)] = (overlap + frame(other_v[...], 0)).astype(BF16)
    for copy in swaps + passing:
        copy.wait_send()
    first.wait_send()
    whole(send2, got2, send_sem.at[1], recv1).wait_send()


def on_device(signal, fan_mask):
    far = pl.BlockSpec(memory_space=pltpu.HBM)
    block = (LINES, ROWS, LINES)
    dma = pltpu.SemaphoreType.DMA
    vmem = pltpu.VMEM
    return pl.pallas_call(
        kernel,
        out_shape=jax.ShapeDtypeStruct(signal.shape, BF16),
        in_specs=[far] * 7,
        out_specs=pl.BlockSpec(memory_space=pltpu.VMEM),
        scratch_shapes=[
            vmem(signal.shape, BF16),
            vmem((LINES, LINES), jnp.int32),
            vmem((3, QUARTER, 2 * BAND), BF16),
            vmem((3, 2 * BAND, QUARTER), BF16),
            vmem((1, WINDOW), F32),
            vmem((4, 2 * LINES, 2 * LINES), BF16),
            vmem((4, LINES, LINES), F32),
            vmem((LAYERS, LINES, LINES), F32),
            vmem((LAYERS, LINES, LINES), BF16),
            vmem((LAYERS, LINES, LINES), BF16),
            vmem(block, BF16),
            vmem(block, BF16),
            vmem(block, BF16),
            vmem(block, BF16),
            vmem(block, BF16),
            vmem((ROWS * LINES, LINES), F32),
            vmem((LINES, 2 * BAND), BF16),
            vmem((LINES, 2 * BAND), BF16),
            dma((5,)),
            dma((6,)),
            dma((LAYERS,)),
            dma((LAYERS,)),
            dma((2,)),
            dma(()),
            dma((LAYERS,)),
            dma((LAYERS,)),
            dma((LAYERS,)),
        ],
        compiler_params=pltpu.CompilerParams(
            collective_id=0, has_side_effects=True, vmem_limit_bytes=56 * 2**20
        ),
        cost_estimate=pl.CostEstimate(
            flops=5 * 10**9, bytes_accessed=20 * 10**6, transcendentals=0
        ),
    )(signal, fan_mask, *tables())


def solution(mesh):
    return jax.shard_map(
        on_device,
        mesh=mesh,
        in_specs=(P("chan", "tm"), P()),
        out_specs=P("chan", "tm"),
        check_vma=False,
    )
```

time: 53.7 us -> 47.5 us (0.88)
  local copies, waits for them, and re-layouts: 5.56 us -> 2.06 us
  Pallas kernels: 47.9 us -> 45.3 us
    unnamed x11 -> x1, local copies, waits for them, and re-layouts: 5.56 us -> 2.06 us
    pallas_call x1, Pallas kernels: 47.9 us -> 45.3 us  [on_device(): pl.pallas_call(kernel, out_shape=jax.ShapeDtypeStruct(signal.shape, BF16)...]
where the time goes in v2:
time: 47.5 us; the launch traced here: 47.4 us
  Pallas kernels  45.3 us (95%)
  local copies, waits for them, and re-layouts  2.06 us (4%)
    pallas_call x1, Pallas kernels, on_device(): pl.pallas_call(kernel, out_shape=jax.ShapeDtypeStruct(signal.shape, BF16)...  45.3 us
    unnamed x1, local copies, waits for them, and re-layouts  2.06 us

profile of v2, /device:TPU:1, one launch (start us, length us, event | category | flops | bytes accessed | tf_op | source)
XLA Modules:
  0.0 47.4 jit_solution(16212672362283542183)
XLA Ops:
  0.0 45.3 %shard_map.73 = bf16[128,3072]{1,0:T(8,128)(2,1)} custom-call(bf16[128,3072]{1,0:T(8,128)(2,1)} %signal.1, s32[128,128]{1,0:T(8,128)} %mask.1, bf16[4,1024,1024]{2,1,0:T(8,128)(2,1)} %constant.10.clone.forward, bf16[4,1024,1024]{2,1,0:T(8,128)(2,1)} %constant.11.clone.inverse, f32[1,4096]{1,0:T(1,128)} %constant.12.clone.taper, ...), custom_call_target="tpu_custom_call" | custom-call | flops 5000000000 | bytes 20000000 | tf_op jit(solution)/shard_map/pallas_call | solution.py:266
  45.3 2.1 %copy.9 = bf16[128,3072]{1,0:T(8,128)(2,1)} copy(bf16[128,3072]{1,0:T(8,128)(2,1)} %shard_map.73) | data formatting | bytes 1572864

commit v3 on v2

v3 whole, which is shorter than its diff:
```python
import functools
import math

import jax
import jax.numpy as jnp
import ml_dtypes
import numpy as np
from jax import lax
from jax.experimental import pallas as pl
from jax.experimental.pallas import tpu as pltpu
from jax.sharding import PartitionSpec as P

WINDOW = 4096
BAND = 512
QUARTER = WINDOW // 4
LINES = 128
BINS = 4
ROWS = 2 * BINS
MESH = pl.DeviceIdType.MESH
F32 = jnp.float32
BF16 = jnp.bfloat16


def high_low(table):
    high = table.astype(ml_dtypes.bfloat16)
    low = (table - high.astype(np.float64)).astype(ml_dtypes.bfloat16)
    return high, low


@functools.cache
def tables():
    positions = np.arange(WINDOW)
    bins = np.arange(BAND)
    angle = 2.0 * math.pi / WINDOW * (positions[:, None] * bins[None, :] % WINDOW)
    cosine, sine = np.cos(angle), np.sin(angle)
    grid = np.arange(LINES).reshape(2, 4, LAYERS, 2)
    owners = grid.transpose(0, 2, 1, 3).reshape(LINES)
    sources = grid.transpose(2, 1, 3, 0).reshape(LINES)
    forward = np.stack([cosine, -sine], axis=1).reshape(WINDOW, 2, LINES, BINS)[:, :, owners]
    forward = forward.transpose(0, 2, 1, 3).reshape(4, QUARTER, 2 * BAND)
    weight = np.where(bins == 0, 1.0, 2.0)
    inverse = np.stack([weight * cosine, -weight * sine], axis=1)
    inverse = inverse.reshape(WINDOW, 2, LINES, BINS)[:, :, owners]
    inverse = inverse.transpose(2, 1, 3, 0).reshape(2 * BAND, 4, QUARTER).transpose(1, 0, 2)
    taper = (0.5 - 0.5 * np.cos(2.0 * math.pi / WINDOW * positions)).reshape(1, WINDOW)
    lines = np.arange(LINES)
    angle = 2.0 * math.pi / LINES * (lines[:, None] * lines[None, :] % LINES)
    cosine, sine = np.cos(angle), np.sin(angle)
    order = np.r_[sources, LINES + sources]
    analysis = np.block([[cosine, sine], [-sine, cosine]])[:, order]
    synthesis = np.block([[cosine, -sine], [sine, cosine]])[order] / LINES
    turns = np.stack(high_low(analysis) + high_low(synthesis))
    angle = 2.0 * math.pi / LINES**2 * (lines[:, None] * lines[None, :])
    fine = np.stack([np.cos(angle), np.sin(angle), cosine, sine]).astype(np.float32)
    return (
        forward.astype(ml_dtypes.bfloat16),
        inverse.astype(ml_dtypes.bfloat16),
        taper.astype(np.float32),
        turns,
        fine,
    )


LAYERS = 8
AROUND = 8
PLANE = LAYERS * AROUND
Z_STEPS = (4, 3, 5, 2, 6, 1, 7, 0)
Y_STEPS = ((2, 1), (2, 0), (1, 1), (3, 1), (1, 0), (3, 0), (0, 1), (0, 0))


def kernel(
    signal, mask, forward, inverse, taper, turns, fine, out,
    sig, mask_v, fwd, inv, taper_v, turns_v, fine_v, own_part, own_send, other_part, summands,
    send1, got1, send2, got2, passed, lines_v, back_v, other_v,
    local, table_sem, sum_send, sum_recv, send_sem, recv1, recv2, pass_send, pass_recv,
):
    me, tm = lax.axis_index("chan"), lax.axis_index("tm")
    rem, div = lax.rem, lax.div
    core, z, y, x = rem(me, 2), rem(div(me, 2), 8), rem(div(me, 16), 4), div(me, 64)
    layers = [rem(z + k, LAYERS) for k in Z_STEPS]
    spots = [(rem(y + j, 4), rem(core + c, 2)) for j, c in Y_STEPS]
    here = (z * 4 + y) * 2 + core
    across = me + PLANE * (1 - 2 * x)
    partner, far, diagonal = {"tm": 1 - tm}, {"chan": across}, {"chan": across, "tm": 1 - tm}

    everyone = []
    for k, layer in enumerate(layers):
        group = spots if Z_STEPS[k] else spots[:-1]
        everyone.append([((layer * 4 + j) * 2 + c, ((x * 4 + j) * 8 + layer) * 2 + c) for j, c in group])

    barrier = pltpu.get_barrier_semaphore()
    for peer in (far, diagonal, partner):
        pl.semaphore_signal(barrier, 1, device_id=peer, device_id_type=MESH)
    for group in everyone:
        for _, d in group:
            pl.semaphore_signal(barrier, 1, device_id={"chan": d}, device_id_type=MESH)

    small = [(signal, sig), (taper, taper_v), (mask, mask_v), (fine, fine_v), (turns, turns_v)]
    small = [pltpu.make_async_copy(a, b, local.at[i]) for i, (a, b) in enumerate(small)]
    edge = 3 * tm
    quarters = [edge, 1, 2]
    fwd_copies = [pltpu.make_async_copy(forward.at[q], fwd.at[i], table_sem.at[i]) for i, q in enumerate(quarters)]
    inv_copies = [pltpu.make_async_copy(inverse.at[q], inv.at[i], table_sem.at[3 + i]) for i, q in enumerate(quarters)]
    for copy in small[:2] + fwd_copies + small[2:] + inv_copies:
        copy.start()

    outer = pl.multiple_of(2 * QUARTER * tm, QUARTER)
    shared = pl.multiple_of(2 * QUARTER * (1 - tm), QUARTER)

    def tapered(offset, quarter):
        weights = taper_v[:, pl.ds(pl.multiple_of(quarter * QUARTER, QUARTER), QUARTER)]
        return (sig[:, pl.ds(offset, QUARTER)].astype(F32) * weights).astype(BF16)

    shape = (2, LAYERS, AROUND * ROWS, LINES)
    small[0].wait()
    small[1].wait()
    both = jnp.concatenate([tapered(shared, edge), tapered(outer, edge)], axis=0)
    fwd_copies[0].wait()
    both = jnp.dot(both, fwd[0], preferred_element_type=F32)
    other_part[...] = both[:LINES].T.reshape(shape).astype(BF16)
    middle = [pl.multiple_of(QUARTER * (1 - tm), QUARTER), pl.multiple_of(QUARTER * (2 - tm), QUARTER)]
    total = both[LINES:]
    for i in range(2):
        fwd_copies[1 + i].wait()
        total += jnp.dot(tapered(middle[i], 1 + i), fwd[1 + i], preferred_element_type=F32)
    own_part[...] = total.T.reshape(shape)
    own_send[...] = own_part[1 - x].astype(BF16)

    pl.semaphore_wait(barrier, PLANE + 2)
    sums = []
    for k, layer in enumerate(layers):
        sources = (other_part.at[x, layer], own_send.at[layer], other_part.at[1 - x, layer])
        sums.append(
            [
                pltpu.make_async_remote_copy(
                    source, summands.at[i, layer], sum_send, sum_recv.at[i, k],
                    device_id=peer, device_id_type=MESH,
                )
                for i, (source, peer) in enumerate(zip(sources, (partner, far, diagonal)))
            ]
        )
        for i in (1, 2, 0):
            sums[k][i].start()

    for k, layer in enumerate(layers):
        for copy in sums[k]:
            copy.wait_recv()
        block = pl.ds(layer * AROUND, AROUND)
        mine = own_part[x, layer] + summands[0, layer].astype(F32)
        theirs = summands[1, layer].astype(F32) + summands[2, layer].astype(F32)
        send1[block, x] = mine.reshape(AROUND, ROWS, LINES).astype(BF16)
        send1[block, 1 - x] = theirs.reshape(AROUND, ROWS, LINES).astype(BF16)
        for place, d in everyone[k]:
            pltpu.make_async_remote_copy(
                send1.at[place], got1.at[here], send_sem.at[0], recv1,
                device_id={"chan": d}, device_id_type=MESH,
            ).start()
    got1[here] = send1[here]

    for copy in small[2:]:
        copy.wait()
    passes = mask_v[pl.ds(me, 1), :].astype(F32) * (1.0 / LINES)
    cosine, sine = fine_v[2], fine_v[3]
    left = jnp.concatenate([cosine * passes, sine * passes], axis=1)
    right = jnp.concatenate(
        [jnp.concatenate([cosine, sine], axis=1), jnp.concatenate([sine, -cosine], axis=1)], axis=0
    )
    fan = jnp.dot(left, right, precision=lax.Precision.HIGHEST, preferred_element_type=F32)
    fan = jnp.concatenate(
        [fan, jnp.concatenate([-fan[:, LINES:], fan[:, :LINES]], axis=1)], axis=0
    )
    fan_high = fan.astype(BF16)
    fan_low = (fan - fan_high.astype(F32)).astype(BF16)

    rest = pl.ds(0, PLANE - 1)
    first = pltpu.make_async_remote_copy(
        send1.at[rest], got1.at[rest], send_sem.at[0], recv1, device_id=partner, device_id_type=MESH
    )
    first.wait_recv()
    lines_v[...] = got1[...].astype(F32).reshape(ROWS * LINES, LINES)
    picked = [lines_v[pl.ds(r, LINES, stride=ROWS), :].astype(BF16) for r in range(ROWS)]
    stacked = jnp.concatenate(
        [jnp.concatenate(picked[:BINS], axis=1), jnp.concatenate(picked[BINS:], axis=1)], axis=0
    )
    wave = jnp.dot(turns_v[0], stacked, preferred_element_type=F32)
    wave += jnp.dot(turns_v[1], stacked, preferred_element_type=F32)
    twist_cos, twist_sin = fine_v[0], fine_v[1]
    turned = []
    for j in range(BINS):
        re = wave[:LINES, j * LINES : (j + 1) * LINES]
        im = wave[LINES:, j * LINES : (j + 1) * LINES]
        turned.append(
            jnp.concatenate(
                [re * twist_cos + im * twist_sin, im * twist_cos - re * twist_sin], axis=1
            )
        )
    turned = jnp.concatenate(turned, axis=0)
    high = turned.astype(BF16)
    low = (turned - high.astype(F32)).astype(BF16)
    masked = jnp.dot(high, fan_high, preferred_element_type=F32)
    masked += jnp.dot(low, fan_high, preferred_element_type=F32)
    masked += jnp.dot(high, fan_low, preferred_element_type=F32)
    real, imag = [], []
    for j in range(BINS):
        re = masked[j * LINES : (j + 1) * LINES, :LINES]
        im = masked[j * LINES : (j + 1) * LINES, LINES:]
        real.append(re * twist_cos - im * twist_sin)
        imag.append(im * twist_cos + re * twist_sin)
    straight = jnp.concatenate(
        [jnp.concatenate(real, axis=1), jnp.concatenate(imag, axis=1)], axis=0
    )
    high = straight.astype(BF16)
    low = (straight - high.astype(F32)).astype(BF16)
    back = jnp.dot(turns_v[2], high, preferred_element_type=F32)
    back += jnp.dot(turns_v[2], low, preferred_element_type=F32)
    back += jnp.dot(turns_v[3], high, preferred_element_type=F32)
    for r in range(ROWS):
        top, column = r // BINS * LINES, r % BINS * LINES
        lines_v[pl.ds(r, LINES, stride=ROWS), :] = back[top : top + LINES, column : column + LINES]
    send2[...] = lines_v[...].reshape(PLANE, 2, ROWS, LINES).astype(BF16)

    halves = (1 - x, x)
    for i, half in enumerate(halves):
        for group in everyone:
            for place, d in group:
                pltpu.make_async_remote_copy(
                    send2.at[place, half], got2.at[half, here], send_sem.at[1], recv2.at[i, z],
                    device_id={"chan": d}, device_id_type=MESH,
                ).start()
        got2[half, here] = send2[here, half]

    for i, half in enumerate(halves):
        for k, layer in enumerate(layers):
            count = got2.at[half, pl.ds(0, len(everyone[k]))]
            pltpu.make_async_remote_copy(
                count, count, send_sem.at[1], recv2.at[i, layer],
                device_id=partner, device_id_type=MESH,
            ).wait_recv()
            block = pl.ds(layer * AROUND, AROUND)
            for kind, peer in ((1, far), (2, diagonal)) if i == 0 else ((0, partner),):
                pltpu.make_async_remote_copy(
                    got2.at[half, block], passed.at[kind, block], pass_send, pass_recv.at[kind],
                    device_id=peer, device_id_type=MESH,
                ).start()

    def turn(block, target, half):
        lines = block.astype(F32).reshape(BAND, LINES).T
        target[:, pl.ds(pl.multiple_of(half * BAND, BAND), BAND)] = lines.astype(BF16)

    def arrived(kind):
        pltpu.make_async_remote_copy(
            passed.at[kind], passed.at[kind], pass_send, pass_recv.at[kind],
            device_id=partner, device_id_type=MESH,
        ).wait_recv()
        return passed[kind]

    def frame(values, i):
        return jnp.dot(values, inv[i], preferred_element_type=F32) * (1.0 / WINDOW)

    turn(got2[x], back_v, x)
    for copy in inv_copies:
        copy.wait()
    turn(arrived(1), back_v, 1 - x)
    out[:, pl.ds(outer, QUARTER)] = frame(back_v[...], 0).astype(BF16)
    centre = 1 + tm
    out[:, QUARTER : 2 * QUARTER] = frame(back_v[...], centre).astype(BF16)
    overlap = frame(back_v[...], 2 - tm)
    turn(arrived(2), other_v, 1 - x)
    turn(arrived(0), other_v, x)
    out[:, pl.ds(shared, QUARTER)] = (overlap + frame(other_v[...], 0)).astype(BF16)

    def sent(ref, sem):
        pltpu.make_async_remote_copy(
            ref, ref, sem, recv1, device_id=partner, device_id_type=MESH
        ).wait_send()

    sent(summands, sum_send)
    first.wait_send()
    sent(send2.at[rest], send_sem.at[1])
    sent(passed, pass_send)


def on_device(signal, fan_mask):
    far = pl.BlockSpec(memory_space=pltpu.HBM)
    block = (PLANE, 2, ROWS, LINES)
    spectra = (LAYERS, AROUND * ROWS, LINES)
    dma = pltpu.SemaphoreType.DMA
    vmem = pltpu.VMEM
    return pl.pallas_call(
        kernel,
        out_shape=jax.ShapeDtypeStruct(signal.shape, BF16),
        in_specs=[far] * 7,
        out_specs=pl.BlockSpec(memory_space=pltpu.VMEM),
        scratch_shapes=[
            vmem(signal.shape, BF16),
            vmem((LINES, LINES), jnp.int32),
            vmem((3, QUARTER, 2 * BAND), BF16),
            vmem((3, 2 * BAND, QUARTER), BF16),
            vmem((1, WINDOW), F32),
            vmem((4, 2 * LINES, 2 * LINES), BF16),
            vmem((4, LINES, LINES), F32),
            vmem((2, *spectra), F32),
            vmem(spectra, BF16),
            vmem((2, *spectra), BF16),
            vmem((3, *spectra), BF16),
            vmem(block, BF16),
            vmem(block, BF16),
            vmem(block, BF16),
            vmem((2, PLANE, ROWS, LINES), BF16),
            vmem((3, PLANE, ROWS, LINES), BF16),
            vmem((ROWS * LINES, LINES), F32),
            vmem((LINES, 2 * BAND), BF16),
            vmem((LINES, 2 * BAND), BF16),
            dma((5,)),
            dma((6,)),
            dma(()),
            dma((3, LAYERS)),
            dma((2,)),
            dma(()),
            dma((2, LAYERS)),
            dma(()),
            dma((3,)),
        ],
        compiler_params=pltpu.CompilerParams(
            collective_id=0, has_side_effects=True, vmem_limit_bytes=56 * 2**20
        ),
        cost_estimate=pl.CostEstimate(
            flops=5 * 10**9, bytes_accessed=20 * 10**6, transcendentals=0
        ),
    )(signal, fan_mask, *tables())


def solution(mesh):
    return jax.shard_map(
        on_device,
        mesh=mesh,
        in_specs=(P("chan", "tm"), P()),
        out_specs=P("chan", "tm"),
        check_vma=False,
    )
```

time: 47.5 us -> 43.6 us (0.918)
  Pallas kernels: 45.3 us -> 41.4 us
    pallas_call x1, Pallas kernels: 45.3 us -> 41.4 us  [on_device(): pl.pallas_call(kernel, out_shape=jax.ShapeDtypeStruct(signal.shape, BF16)...]
where the time goes in v3:
time: 43.6 us; the launch traced here: 43.5 us
  Pallas kernels  41.4 us (95%)
  local copies, waits for them, and re-layouts  2.06 us (5%)
    pallas_call x1, Pallas kernels, on_device(): pl.pallas_call(kernel, out_shape=jax.ShapeDtypeStruct(signal.shape, BF16)...  41.4 us
    unnamed x1, local copies, waits for them, and re-layouts  2.06 us

profile of v3, /device:TPU:1, one launch (start us, length us, event | category | flops | bytes accessed | tf_op | source)
XLA Modules:
  0.0 43.5 jit_solution(6329847474667054931)
XLA Ops:
  0.0 41.4 %shard_map.73 = bf16[128,3072]{1,0:T(8,128)(2,1)} custom-call(bf16[128,3072]{1,0:T(8,128)(2,1)} %signal.1, s32[128,128]{1,0:T(8,128)} %mask.1, bf16[4,1024,1024]{2,1,0:T(8,128)(2,1)} %constant.10.clone.forward, bf16[4,1024,1024]{2,1,0:T(8,128)(2,1)} %constant.11.clone.inverse, f32[1,4096]{1,0:T(1,128)} %constant.12.clone.taper, ...), custom_call_target="tpu_custom_call" | custom-call | flops 5000000000 | bytes 20000000 | tf_op jit(solution)/shard_map/pallas_call | solution.py:289
  41.4 2.1 %copy.9 = bf16[128,3072]{1,0:T(8,128)(2,1)} copy(bf16[128,3072]{1,0:T(8,128)(2,1)} %shard_map.73) | data formatting | bytes 1572864

commit v4 on v3

v4 whole, which is shorter than its diff:
```python
import functools
import math

import jax
import jax.numpy as jnp
import ml_dtypes
import numpy as np
from jax import lax
from jax.experimental import pallas as pl
from jax.experimental.pallas import tpu as pltpu
from jax.sharding import PartitionSpec as P

WINDOW = 4096
BAND = 512
QUARTER = WINDOW // 4
LINES = 128
BINS = 4
PAIR = BINS // 2
ROWS = 2 * BINS
MESH = pl.DeviceIdType.MESH
F32 = jnp.float32
BF16 = jnp.bfloat16


def high_low(table):
    high = table.astype(ml_dtypes.bfloat16)
    low = (table - high.astype(np.float64)).astype(ml_dtypes.bfloat16)
    return high, low


@functools.cache
def tables():
    positions = np.arange(WINDOW)
    bins = np.arange(BAND)
    angle = 2.0 * math.pi / WINDOW * (positions[:, None] * bins[None, :] % WINDOW)
    cosine, sine = np.cos(angle), np.sin(angle)
    grid = np.arange(LINES).reshape(2, 4, LAYERS, 2)
    owners = grid.transpose(0, 2, 1, 3).reshape(LINES)
    places = [(WINDOW, 2, 2, PLANE, 2, PAIR), (0, 2, 4, 3, 1, 5)]
    forward = np.stack([cosine, -sine], axis=1).reshape(WINDOW, 2, LINES, BINS)[:, :, owners]
    forward = forward.reshape(places[0]).transpose(places[1]).reshape(4, QUARTER, 2 * BAND)
    weight = np.where(bins == 0, 1.0, 2.0)
    inverse = np.stack([weight * cosine, -weight * sine], axis=1)
    inverse = inverse.reshape(WINDOW, 2, LINES, BINS)[:, :, owners]
    inverse = inverse.reshape(places[0]).transpose(places[1]).reshape(4, QUARTER, 2 * BAND)
    inverse = inverse.transpose(0, 2, 1)
    taper = (0.5 - 0.5 * np.cos(2.0 * math.pi / WINDOW * positions)).reshape(1, WINDOW)
    lines = np.arange(LINES)
    angle = 2.0 * math.pi / LINES * (lines[:, None] * lines[None, :] % LINES)
    cosine, sine = np.cos(angle), np.sin(angle)
    order = np.r_[owners, LINES + owners]
    analysis = np.block([[cosine, sine], [-sine, cosine]])[:, order]
    synthesis = np.block([[cosine, -sine], [sine, cosine]])[order] / LINES
    turns = np.stack(high_low(analysis) + high_low(synthesis))
    angle = 2.0 * math.pi / LINES**2 * (lines[:, None] * lines[None, :])
    fine = np.stack([np.cos(angle), np.sin(angle), cosine, sine]).astype(np.float32)
    return (
        forward.astype(ml_dtypes.bfloat16),
        inverse.astype(ml_dtypes.bfloat16),
        taper.astype(np.float32),
        turns,
        fine,
    )


LAYERS = 8
AROUND = 8
PLANE = LAYERS * AROUND
GROUP = AROUND * 2 * PAIR
Z_STEPS = (4, 3, 5, 2, 6, 1, 7, 0)
AHEAD = 8
Y_STEPS = ((2, 1), (2, 0), (1, 1), (3, 1), (1, 0), (3, 0), (0, 1), (0, 0))


def regroup(first, second):
    upper = jnp.concatenate([first[:, :4], second[:, :4]], axis=1)
    return upper, jnp.concatenate([first[:, 4:], second[:, 4:]], axis=1)


def kernel(
    signal, mask, forward, inverse, taper, turns, fine, out,
    sig, mask_v, fwd, inv, taper_v, turns_v, fine_v, own_part, own_send, other_part, summands,
    send1, got1, send2, got2, kept, leaving, passed, lines_v, back_v, other_v,
    local, table_sem, sum_send, sum_recv, send_sem, recv1, recv2, pass_send, pass_recv,
):
    me, tm = lax.axis_index("chan"), lax.axis_index("tm")
    rem, div = lax.rem, lax.div
    core, z, y, x = rem(me, 2), rem(div(me, 2), 8), rem(div(me, 16), 4), div(me, 64)
    layers = [rem(z + k, LAYERS) for k in Z_STEPS]
    spots = [(rem(y + j, 4), rem(core + c, 2)) for j, c in Y_STEPS]
    here = (z * 4 + y) * 2 + core
    across = me + PLANE * (1 - 2 * x)
    partner, far, diagonal = {"tm": 1 - tm}, {"chan": across}, {"chan": across, "tm": 1 - tm}

    everyone = []
    for k, layer in enumerate(layers):
        group = spots if Z_STEPS[k] else spots[:-1]
        everyone.append([((layer * 4 + j) * 2 + c, ((x * 4 + j) * 8 + layer) * 2 + c) for j, c in group])

    barrier = pltpu.get_barrier_semaphore()
    for peer in (far, diagonal, partner):
        pl.semaphore_signal(barrier, 1, device_id=peer, device_id_type=MESH)
    for group in everyone:
        for _, d in group:
            pl.semaphore_signal(barrier, 1, device_id={"chan": d}, device_id_type=MESH)

    small = [(signal, sig), (taper, taper_v), (mask, mask_v), (fine, fine_v), (turns, turns_v)]
    small = [pltpu.make_async_copy(a, b, local.at[i]) for i, (a, b) in enumerate(small)]
    edge = 3 * tm
    quarters = [edge, 1, 2]
    fwd_copies = [pltpu.make_async_copy(forward.at[q], fwd.at[i], table_sem.at[i]) for i, q in enumerate(quarters)]
    inv_copies = [pltpu.make_async_copy(inverse.at[q], inv.at[i], table_sem.at[3 + i]) for i, q in enumerate(quarters)]
    for copy in small[:2] + fwd_copies + small[2:] + inv_copies:
        copy.start()

    outer = pl.multiple_of(2 * QUARTER * tm, QUARTER)
    shared = pl.multiple_of(2 * QUARTER * (1 - tm), QUARTER)

    def tapered(offset, quarter):
        weights = taper_v[:, pl.ds(pl.multiple_of(quarter * QUARTER, QUARTER), QUARTER)]
        return (sig[:, pl.ds(offset, QUARTER)].astype(F32) * weights).astype(BF16)

    shape = (2, 2, LAYERS, GROUP, LINES)
    small[0].wait()
    small[1].wait()
    both = jnp.concatenate([tapered(shared, edge), tapered(outer, edge)], axis=0)
    fwd_copies[0].wait()
    both = jnp.dot(both, fwd[0], preferred_element_type=F32)
    other_part[...] = both[:LINES].T.reshape(shape).astype(BF16)
    middle = [pl.multiple_of(QUARTER * (1 - tm), QUARTER), pl.multiple_of(QUARTER * (2 - tm), QUARTER)]
    total = both[LINES:]
    for i in range(2):
        fwd_copies[1 + i].wait()
        total += jnp.dot(tapered(middle[i], 1 + i), fwd[1 + i], preferred_element_type=F32)
    own_part[...] = total.T.reshape(shape)
    own_send[...] = own_part[1 - x].astype(BF16)

    pl.semaphore_wait(barrier, PLANE + 2)
    sums = []
    for pair in range(2):
        for k, layer in enumerate(layers):
            sources = (other_part.at[x, pair, layer], own_send.at[pair, layer], other_part.at[1 - x, pair, layer])
            sums.append(
                [
                    pltpu.make_async_remote_copy(
                        source, summands.at[i, pair, layer], sum_send, sum_recv.at[pair, i, k],
                        device_id=peer, device_id_type=MESH,
                    )
                    for i, (source, peer) in enumerate(zip(sources, (partner, far, diagonal)))
                ]
            )
            if pair * LAYERS + k < AHEAD:
                for i in (1, 2, 0):
                    sums[-1][i].start()

    def spread(source, target, pair, group, send, recv):
        for place, d in group:
            pltpu.make_async_remote_copy(
                source.at[pair, place], target.at[pair, here], send, recv,
                device_id={"chan": d}, device_id_type=MESH,
            ).start()

    def rows(tiles):
        return tiles.reshape(AROUND // 2, ROWS, LINES)

    for pair in range(2):
        for k, layer in enumerate(layers):
            step = pair * LAYERS + k
            for copy in sums[step]:
                copy.wait_recv()
            if step + AHEAD < 2 * LAYERS:
                for i in (1, 2, 0):
                    sums[step + AHEAD][i].start()
            mine = own_part[x, pair, layer] + summands[0, pair, layer].astype(F32)
            theirs = summands[1, pair, layer].astype(F32) + summands[2, pair, layer].astype(F32)
            low, high = jnp.where(x == 0, mine, theirs), jnp.where(x == 0, theirs, mine)
            even, odd = regroup(rows(low), rows(high))
            tiles = jnp.stack([even, odd], axis=1).reshape(AROUND, ROWS, LINES)
            send1[pair, pl.ds(layer * AROUND, AROUND)] = tiles.astype(BF16)
            spread(send1, got1, pair, everyone[k], send_sem.at[0], recv1.at[pair])
        got1[pair, here] = send1[pair, here]

    for copy in small[2:]:
        copy.wait()
    passes = mask_v[pl.ds(me, 1), :].astype(F32) * (1.0 / LINES)
    cosine, sine = fine_v[2], fine_v[3]
    left = jnp.concatenate([cosine * passes, sine * passes], axis=1)
    right = jnp.concatenate(
        [jnp.concatenate([cosine, sine], axis=1), jnp.concatenate([sine, -cosine], axis=1)], axis=0
    )
    fan = jnp.dot(left, right, precision=lax.Precision.HIGHEST, preferred_element_type=F32)
    fan = jnp.concatenate(
        [fan, jnp.concatenate([-fan[:, LINES:], fan[:, :LINES]], axis=1)], axis=0
    )
    fan_high = fan.astype(BF16)
    fan_low = (fan - fan_high.astype(F32)).astype(BF16)

    twist_cos, twist_sin = fine_v[0], fine_v[1]

    def across_channels(pair):
        lines = lines_v.at[pair]
        lines[...] = got1[pair].astype(F32).reshape(PLANE * ROWS, LINES)

        def spot(half, imag, b):
            return pl.ds(half * ROWS // 2 + imag * PAIR + b, PLANE, stride=ROWS)

        picked = [
            [
                jnp.concatenate([lines[spot(h, imag, b), :] for h in range(2)], axis=0).astype(BF16)
                for b in range(PAIR)
            ]
            for imag in range(2)
        ]
        stacked = jnp.concatenate([jnp.concatenate(p, axis=1) for p in picked], axis=0)
        wave = jnp.dot(turns_v[0], stacked, preferred_element_type=F32)
        wave += jnp.dot(turns_v[1], stacked, preferred_element_type=F32)
        turned = []
        for b in range(PAIR):
            re = wave[:LINES, b * LINES : (b + 1) * LINES]
            im = wave[LINES:, b * LINES : (b + 1) * LINES]
            turned.append(
                jnp.concatenate(
                    [re * twist_cos + im * twist_sin, im * twist_cos - re * twist_sin], axis=1
                )
            )
        turned = jnp.concatenate(turned, axis=0)
        high = turned.astype(BF16)
        low = (turned - high.astype(F32)).astype(BF16)
        masked = jnp.dot(high, fan_high, preferred_element_type=F32)
        masked += jnp.dot(low, fan_high, preferred_element_type=F32)
        masked += jnp.dot(high, fan_low, preferred_element_type=F32)
        real, imag = [], []
        for b in range(PAIR):
            re = masked[b * LINES : (b + 1) * LINES, :LINES]
            im = masked[b * LINES : (b + 1) * LINES, LINES:]
            real.append(re * twist_cos - im * twist_sin)
            imag.append(im * twist_cos + re * twist_sin)
        straight = jnp.concatenate(
            [jnp.concatenate(real, axis=1), jnp.concatenate(imag, axis=1)], axis=0
        )
        high = straight.astype(BF16)
        low = (straight - high.astype(F32)).astype(BF16)
        back = jnp.dot(turns_v[2], high, preferred_element_type=F32)
        back += jnp.dot(turns_v[2], low, preferred_element_type=F32)
        back += jnp.dot(turns_v[3], high, preferred_element_type=F32)
        for h in range(2):
            for i in range(2):
                top = i * LINES + h * PLANE
                for b in range(PAIR):
                    lines[spot(h, i, b), :] = back[top : top + PLANE, b * LINES : (b + 1) * LINES]
        send2[pair] = lines[...].reshape(PLANE, ROWS, LINES).astype(BF16)

    rest = pl.ds(0, PLANE - 1)

    def transfer(ref, send, recv):
        return pltpu.make_async_remote_copy(
            ref, ref, send, recv, device_id=partner, device_id_type=MESH
        )

    for pair in range(2):
        transfer(got1.at[pair, rest], send_sem.at[0], recv1.at[pair]).wait_recv()
        across_channels(pair)
        for group in everyone:
            spread(send2, got2, pair, group, send_sem.at[1], recv2.at[pair, z])
        got2[pair, here] = send2[pair, here]

    for pair in range(2):
        for k, layer in enumerate(layers):
            count = pl.ds(0, len(everyone[k]))
            transfer(got2.at[pair, count], send_sem.at[1], recv2.at[pair, layer]).wait_recv()
            tiles = got2[pair, pl.ds(layer * AROUND, AROUND)].astype(F32)
            tiles = tiles.reshape(AROUND // 2, 2, ROWS, LINES)
            low, high = regroup(tiles[:, 0], tiles[:, 1])
            mine, theirs = jnp.where(x == 0, low, high), jnp.where(x == 0, high, low)
            kept[pair, layer] = mine.reshape(GROUP, LINES).astype(BF16)
            leaving[pair, layer] = theirs.reshape(GROUP, LINES).astype(BF16)
            for kind, source, peer in ((1, leaving, far), (2, leaving, diagonal), (0, kept, partner)):
                pltpu.make_async_remote_copy(
                    source.at[pair, layer], passed.at[kind, pair, layer], pass_send,
                    pass_recv.at[kind, pair], device_id=peer, device_id_type=MESH,
                ).start()

    def turn(block, target, half, pair):
        lines = block.astype(F32).reshape(BAND // 2, LINES).T
        column = half * BAND + pair * (BAND // 2)
        target[:, pl.ds(pl.multiple_of(column, BAND // 2), BAND // 2)] = lines.astype(BF16)

    def arrived(kind, target, half, pair):
        transfer(passed.at[kind, pair], pass_send, pass_recv.at[kind, pair]).wait_recv()
        turn(passed[kind, pair], target, half, pair)

    def frame(values, i):
        return jnp.dot(values, inv[i], preferred_element_type=F32) * (1.0 / WINDOW)

    for copy in inv_copies:
        copy.wait()
    for pair in range(2):
        turn(kept[pair], back_v, x, pair)
        arrived(1, back_v, 1 - x, pair)
    out[:, pl.ds(outer, QUARTER)] = frame(back_v[...], 0).astype(BF16)
    centre = 1 + tm
    out[:, QUARTER : 2 * QUARTER] = frame(back_v[...], centre).astype(BF16)
    overlap = frame(back_v[...], 2 - tm)
    for pair in range(2):
        arrived(2, other_v, 1 - x, pair)
        arrived(0, other_v, x, pair)
    out[:, pl.ds(shared, QUARTER)] = (overlap + frame(other_v[...], 0)).astype(BF16)
    transfer(summands, sum_send, recv1.at[0]).wait_send()
    transfer(send1.at[:, rest], send_sem.at[0], recv1.at[0]).wait_send()
    transfer(send2.at[:, rest], send_sem.at[1], recv1.at[0]).wait_send()
    transfer(passed, pass_send, recv1.at[0]).wait_send()


def on_device(signal, fan_mask):
    far = pl.BlockSpec(memory_space=pltpu.HBM)
    block = (2, PLANE, ROWS, LINES)
    spectra = (2, LAYERS, GROUP, LINES)
    dma = pltpu.SemaphoreType.DMA
    vmem = pltpu.VMEM
    return pl.pallas_call(
        kernel,
        out_shape=jax.ShapeDtypeStruct(signal.shape, BF16),
        in_specs=[far] * 7,
        out_specs=pl.BlockSpec(memory_space=pltpu.VMEM),
        scratch_shapes=[
            vmem(signal.shape, BF16),
            vmem((LINES, LINES), jnp.int32),
            vmem((3, QUARTER, 2 * BAND), BF16),
            vmem((3, 2 * BAND, QUARTER), BF16),
            vmem((1, WINDOW), F32),
            vmem((4, 2 * LINES, 2 * LINES), BF16),
            vmem((4, LINES, LINES), F32),
            vmem((2, *spectra), F32),
            vmem(spectra, BF16),
            vmem((2, *spectra), BF16),
            vmem((3, *spectra), BF16),
            vmem(block, BF16),
            vmem(block, BF16),
            vmem(block, BF16),
            vmem(block, BF16),
            vmem(spectra, BF16),
            vmem(spectra, BF16),
            vmem((3, *spectra), BF16),
            vmem((2, PLANE * ROWS, LINES), F32),
            vmem((LINES, 2 * BAND), BF16),
            vmem((LINES, 2 * BAND), BF16),
            dma((5,)),
            dma((6,)),
            dma(()),
            dma((2, 3, LAYERS)),
            dma((2,)),
            dma((2,)),
            dma((2, LAYERS)),
            dma(()),
            dma((3, 2)),
        ],
        compiler_params=pltpu.CompilerParams(
            collective_id=0, has_side_effects=True, vmem_limit_bytes=56 * 2**20
        ),
        cost_estimate=pl.CostEstimate(
            flops=5 * 10**9, bytes_accessed=20 * 10**6, transcendentals=0
        ),
    )(signal, fan_mask, *tables())


def solution(mesh):
    return jax.shard_map(
        on_device,
        mesh=mesh,
        in_specs=(P("chan", "tm"), P()),
        out_specs=P("chan", "tm"),
        check_vma=False,
    )
```

time: 43.6 us -> 42.3 us (0.970)
  Pallas kernels: 41.4 us -> 40.1 us
    pallas_call x1, Pallas kernels: 41.4 us -> 40.1 us  [on_device(): pl.pallas_call(kernel, out_shape=jax.ShapeDtypeStruct(signal.shape, BF16)...]
where the time goes in v4:
time: 42.3 us; the launch traced here: 42.2 us
  Pallas kernels  40.1 us (95%)
  local copies, waits for them, and re-layouts  2.06 us (5%)
    pallas_call x1, Pallas kernels, on_device(): pl.pallas_call(kernel, out_shape=jax.ShapeDtypeStruct(signal.shape, BF16)...  40.1 us
    unnamed x1, local copies, waits for them, and re-layouts  2.06 us

profile of v4, /device:TPU:1, one launch (start us, length us, event | category | flops | bytes accessed | tf_op | source)
XLA Modules:
  0.0 42.2 jit_solution(12641016488499313122)
XLA Ops:
  0.0 40.1 %shard_map.73 = bf16[128,3072]{1,0:T(8,128)(2,1)} custom-call(bf16[128,3072]{1,0:T(8,128)(2,1)} %signal.1, s32[128,128]{1,0:T(8,128)} %mask.1, bf16[4,1024,1024]{2,1,0:T(8,128)(2,1)} %constant.10.clone.forward, bf16[4,1024,1024]{2,1,0:T(8,128)(2,1)} %constant.11.clone.inverse, f32[1,4096]{1,0:T(1,128)} %constant.12.clone.taper, ...), custom_call_target="tpu_custom_call" | custom-call | flops 5000000000 | bytes 20000000 | tf_op jit(solution)/shard_map/pallas_call | solution.py:320
  40.1 2.1 %copy.9 = bf16[128,3072]{1,0:T(8,128)(2,1)} copy(bf16[128,3072]{1,0:T(8,128)(2,1)} %shard_map.73) | data formatting | bytes 1572864

commit v5 on v4

--- a/solution.py
+++ b/solution.py
@@ -26,6 +26,14 @@
     high = table.astype(ml_dtypes.bfloat16)
     low = (table - high.astype(np.float64)).astype(ml_dtypes.bfloat16)
     return high, low
+
+
+def three_parts(table):
+    rest, parts = table.astype(np.float32), []
+    for _ in range(3):
+        parts.append(rest.astype(ml_dtypes.bfloat16))
+        rest = rest - parts[-1].astype(np.float32)
+    return parts
 
 
 @functools.cache
@@ -44,7 +52,7 @@
     inverse = inverse.reshape(WINDOW, 2, LINES, BINS)[:, :, owners]
     inverse = inverse.reshape(places[0]).transpose(places[1]).reshape(4, QUARTER, 2 * BAND)
     inverse = inverse.transpose(0, 2, 1)
-    taper = (0.5 - 0.5 * np.cos(2.0 * math.pi / WINDOW * positions)).reshape(1, WINDOW)
+    taper = (0.5 - 0.5 * np.cos(2.0 * math.pi / WINDOW * positions)).reshape(4, QUARTER)
     lines = np.arange(LINES)
     angle = 2.0 * math.pi / LINES * (lines[:, None] * lines[None, :] % LINES)
     cosine, sine = np.cos(angle), np.sin(angle)
@@ -53,19 +61,19 @@
     synthesis = np.block([[cosine, -sine], [sine, cosine]])[order] / LINES
     turns = np.stack(high_low(analysis) + high_low(synthesis))
     angle = 2.0 * math.pi / LINES**2 * (lines[:, None] * lines[None, :])
-    fine = np.stack([np.cos(angle), np.sin(angle), cosine, sine]).astype(np.float32)
-    return (
-        forward.astype(ml_dtypes.bfloat16),
-        inverse.astype(ml_dtypes.bfloat16),
-        taper.astype(np.float32),
-        turns,
-        fine,
-    )
+    fine = np.stack([np.cos(angle), np.sin(angle), cosine, sine])
+    taper = np.concatenate([np.pad(part, ((0, 12), (0, 0))) for part in three_parts(taper)])
+    blocks = [part[i] for i in range(4) for part in three_parts(fine)] + [np.zeros_like(cosine)] * 4
+    fine = np.concatenate([np.concatenate(blocks[k : k + 8], axis=1) for k in (0, 8)])
+    rows = [taper, fine, np.concatenate(list(turns), axis=1), *forward, *inverse]
+    return np.concatenate([part.astype(ml_dtypes.bfloat16) for part in rows])
 
 
 LAYERS = 8
 AROUND = 8
 PLANE = LAYERS * AROUND
+TAPER_ROWS = 48
+PACKED = TAPER_ROWS + 4 * LINES
 GROUP = AROUND * 2 * PAIR
 Z_STEPS = (4, 3, 5, 2, 6, 1, 7, 0)
 AHEAD = 8
@@ -78,9 +86,9 @@
 
 
 def kernel(
-    signal, mask, forward, inverse, taper, turns, fine, out,
-    sig, mask_v, fwd, inv, taper_v, turns_v, fine_v, own_part, own_send, other_part, summands,
-    send1, got1, send2, got2, kept, leaving, passed, lines_v, back_v, other_v,
+    signal, mask, table, out,
+    sig, mask_v, fwd, inv, packed, taper_v, fine_v, own_part, own_send, other_part, summands,
+    send1, got1, send2, got2, kept, leaving, passed, lines_v, frames,
     local, table_sem, sum_send, sum_recv, send_sem, recv1, recv2, pass_send, pass_recv,
 ):
     me, tm = lax.axis_index("chan"), lax.axis_index("tm")
@@ -104,12 +112,27 @@
         for _, d in group:
             pl.semaphore_signal(barrier, 1, device_id={"chan": d}, device_id_type=MESH)
 
-    small = [(signal, sig), (taper, taper_v), (mask, mask_v), (fine, fine_v), (turns, turns_v)]
-    small = [pltpu.make_async_copy(a, b, local.at[i]) for i, (a, b) in enumerate(small)]
     edge = 3 * tm
     quarters = [edge, 1, 2]
-    fwd_copies = [pltpu.make_async_copy(forward.at[q], fwd.at[i], table_sem.at[i]) for i, q in enumerate(quarters)]
-    inv_copies = [pltpu.make_async_copy(inverse.at[q], inv.at[i], table_sem.at[3 + i]) for i, q in enumerate(quarters)]
+
+    def part_of_table(start, size, target, sem):
+        start = pl.multiple_of(start, 16)
+        return pltpu.make_async_copy(table.at[pl.ds(start, size)], target, sem)
+
+    small = [
+        pltpu.make_async_copy(signal, sig, local.at[0]),
+        part_of_table(0, TAPER_ROWS, packed.at[:TAPER_ROWS], local.at[1]),
+        part_of_table(TAPER_ROWS, PACKED - TAPER_ROWS, packed.at[TAPER_ROWS:], local.at[2]),
+        pltpu.make_async_copy(mask, mask_v, local.at[3]),
+    ]
+    fwd_copies = [
+        part_of_table(PACKED + q * QUARTER, QUARTER, fwd.at[i], table_sem.at[i])
+        for i, q in enumerate(quarters)
+    ]
+    inv_copies = [
+        part_of_table(PACKED + (4 + q) * QUARTER, QUARTER, inv.at[i], table_sem.at[3 + i])
+        for i, q in enumerate(quarters)
+    ]
     for copy in small[:2] + fwd_copies + small[2:] + inv_copies:
         copy.start()
 
@@ -117,12 +140,14 @@
     shared = pl.multiple_of(2 * QUARTER * (1 - tm), QUARTER)
 
     def tapered(offset, quarter):
-        weights = taper_v[:, pl.ds(pl.multiple_of(quarter * QUARTER, QUARTER), QUARTER)]
+        weights = taper_v[pl.ds(quarter, 1), :]
         return (sig[:, pl.ds(offset, QUARTER)].astype(F32) * weights).astype(BF16)
 
     shape = (2, 2, LAYERS, GROUP, LINES)
     small[0].wait()
     small[1].wait()
+    parts = [packed[16 * i : 16 * (i + 1), :].astype(F32) for i in range(3)]
+    taper_v[...] = parts[0] + parts[1] + parts[2]
     both = jnp.concatenate([tapered(shared, edge), tapered(outer, edge)], axis=0)
     fwd_copies[0].wait()
     both = jnp.dot(both, fwd[0], preferred_element_type=F32)
@@ -182,6 +207,13 @@
 
     for copy in small[2:]:
         copy.wait()
+    for i in range(4):
+        parts = []
+        for k in range(3 * i, 3 * i + 3):
+            top, column = TAPER_ROWS + k // 8 * LINES, k % 8 * LINES
+            parts.append(packed[top : top + LINES, column : column + LINES].astype(F32))
+        fine_v[i] = parts[0] + parts[1] + parts[2]
+    turns = [packed[PACKED - 2 * LINES :, 2 * LINES * i : 2 * LINES * (i + 1)] for i in range(4)]
     passes = mask_v[pl.ds(me, 1), :].astype(F32) * (1.0 / LINES)
     cosine, sine = fine_v[2], fine_v[3]
     left = jnp.concatenate([cosine * passes, sine * passes], axis=1)
@@ -212,8 +244,8 @@
             for imag in range(2)
         ]
         stacked = jnp.concatenate([jnp.concatenate(p, axis=1) for p in picked], axis=0)
-        wave = jnp.dot(turns_v[0], stacked, preferred_element_type=F32)
-        wave += jnp.dot(turns_v[1], stacked, preferred_element_type=F32)
+        wave = jnp.dot(turns[0], stacked, preferred_element_type=F32)
+        wave += jnp.dot(turns[1], stacked, preferred_element_type=F32)
         turned = []
         for b in range(PAIR):
             re = wave[:LINES, b * LINES : (b + 1) * LINES]
@@ -240,9 +272,9 @@
         )
         high = straight.astype(BF16)
         low = (straight - high.astype(F32)).astype(BF16)
-        back = jnp.dot(turns_v[2], high, preferred_element_type=F32)
-        back += jnp.dot(turns_v[2], low, preferred_element_type=F32)
-        back += jnp.dot(turns_v[3], high, preferred_element_type=F32)
+        back = jnp.dot(turns[2], high, preferred_element_type=F32)
+        back += jnp.dot(turns[2], low, preferred_element_type=F32)
+        back += jnp.dot(turns[3], high, preferred_element_type=F32)
         for h in range(2):
             for i in range(2):
                 top = i * LINES + h * PLANE
@@ -260,12 +292,12 @@
     for pair in range(2):
         transfer(got1.at[pair, rest], send_sem.at[0], recv1.at[pair]).wait_recv()
         across_channels(pair)
-        for group in everyone:
+        for group in reversed(everyone):
             spread(send2, got2, pair, group, send_sem.at[1], recv2.at[pair, z])
         got2[pair, here] = send2[pair, here]
 
     for pair in range(2):
-        for k, layer in enumerate(layers):
+        for k, layer in reversed(list(enumerate(layers))):
             count = pl.ds(0, len(everyone[k]))
             transfer(got2.at[pair, count], send_sem.at[1], recv2.at[pair, layer]).wait_recv()
             tiles = got2[pair, pl.ds(layer * AROUND, AROUND)].astype(F32)
@@ -280,31 +312,36 @@
                     pass_recv.at[kind, pair], device_id=peer, device_id_type=MESH,
                 ).start()
 
-    def turn(block, target, half, pair):
-        lines = block.astype(F32).reshape(BAND // 2, LINES).T
-        column = half * BAND + pair * (BAND // 2)
-        target[:, pl.ds(pl.multiple_of(column, BAND // 2), BAND // 2)] = lines.astype(BF16)
-
-    def arrived(kind, target, half, pair):
+    places = ((0, 0), (1, 1 + tm), (2, 2 - tm))
+
+    def terms(block, half, pair, quarters):
+        lines = block.astype(F32).reshape(BAND // 2, LINES).T.astype(BF16)
+        rows = pl.ds(pl.multiple_of((2 * half + pair) * (BAND // 2), BAND // 2), BAND // 2)
+        return [jnp.dot(lines, inv[i, rows, :], preferred_element_type=F32) for i in quarters]
+
+    def arrived(kind, pair):
         transfer(passed.at[kind, pair], pass_send, pass_recv.at[kind, pair]).wait_recv()
-        turn(passed[kind, pair], target, half, pair)
-
-    def frame(values, i):
-        return jnp.dot(values, inv[i], preferred_element_type=F32) * (1.0 / WINDOW)
+        return passed[kind, pair]
+
+    def put(column, value):
+        out[:, pl.ds(column, QUARTER)] = (value * (1.0 / WINDOW)).astype(BF16)
 
     for copy in inv_copies:
         copy.wait()
-    for pair in range(2):
-        turn(kept[pair], back_v, x, pair)
-        arrived(1, back_v, 1 - x, pair)
-    out[:, pl.ds(outer, QUARTER)] = frame(back_v[...], 0).astype(BF16)
-    centre = 1 + tm
-    out[:, QUARTER : 2 * QUARTER] = frame(back_v[...], centre).astype(BF16)
-    overlap = frame(back_v[...], 2 - tm)
-    for pair in range(2):
-        arrived(2, other_v, 1 - x, pair)
-        arrived(0, other_v, x, pair)
-    out[:, pl.ds(shared, QUARTER)] = (overlap + frame(other_v[...], 0)).astype(BF16)
+    mine = [i for _, i in places]
+    for k, term in enumerate(terms(kept[0], x, 0, mine)):
+        frames[k] = term
+    for k, term in enumerate(terms(kept[1], x, 1, mine)):
+        frames[k] += term
+    for k, term in enumerate(terms(arrived(1, 0), 1 - x, 0, mine)):
+        frames[k] += term
+    frames[2] += terms(arrived(2, 0), 1 - x, 0, [0])[0] + terms(arrived(0, 0), x, 0, [0])[0]
+    last = terms(arrived(1, 1), 1 - x, 1, mine)
+    put(outer, frames[0] + last[0])
+    put(QUARTER, frames[1] + last[1])
+    frames[2] += last[2]
+    last = terms(arrived(2, 1), 1 - x, 1, [0])[0] + terms(arrived(0, 1), x, 1, [0])[0]
+    put(shared, frames[2] + last)
     transfer(summands, sum_send, recv1.at[0]).wait_send()
     transfer(send1.at[:, rest], send_sem.at[0], recv1.at[0]).wait_send()
     transfer(send2.at[:, rest], send_sem.at[1], recv1.at[0]).wait_send()
@@ -320,15 +357,15 @@
     return pl.pallas_call(
         kernel,
         out_shape=jax.ShapeDtypeStruct(signal.shape, BF16),
-        in_specs=[far] * 7,
+        in_specs=[far] * 3,
         out_specs=pl.BlockSpec(memory_space=pltpu.VMEM),
         scratch_shapes=[
             vmem(signal.shape, BF16),
             vmem((LINES, LINES), jnp.int32),
             vmem((3, QUARTER, 2 * BAND), BF16),
             vmem((3, 2 * BAND, QUARTER), BF16),
-            vmem((1, WINDOW), F32),
-            vmem((4, 2 * LINES, 2 * LINES), BF16),
+            vmem((PACKED, 2 * BAND), BF16),
+            vmem((16, QUARTER), F32),
             vmem((4, LINES, LINES), F32),
             vmem((2, *spectra), F32),
             vmem(spectra, BF16),
@@ -342,9 +379,8 @@
             vmem(spectra, BF16),
             vmem((3, *spectra), BF16),
             vmem((2, PLANE * ROWS, LINES), F32),
-            vmem((LINES, 2 * BAND), BF16),
-            vmem((LINES, 2 * BAND), BF16),
-            dma((5,)),
+            vmem((3, LINES, QUARTER), F32),
+            dma((4,)),
             dma((6,)),
             dma(()),
             dma((2, 3, LAYERS)),
@@ -355,12 +391,12 @@
             dma((3, 2)),
         ],
         compiler_params=pltpu.CompilerParams(
-            collective_id=0, has_side_effects=True, vmem_limit_bytes=56 * 2**20
+            collective_id=0, has_side_effects=True, vmem_limit_bytes=53 * 2**20
         ),
         cost_estimate=pl.CostEstimate(
             flops=5 * 10**9, bytes_accessed=20 * 10**6, transcendentals=0
         ),
-    )(signal, fan_mask, *tables())
+    )(signal, fan_mask, tables())
 
 
 def solution(mesh):

time: 42.3 us -> 39.4 us (0.931)
  Pallas kernels: 40.1 us -> 37.6 us
    pallas_call x1, Pallas kernels: 40.1 us -> 37.6 us  [on_device(): pl.pallas_call(kernel, out_shape=jax.ShapeDtypeStruct(signal.shape, BF16)...]
    unnamed x1 -> x3, local copies, waits for them, and re-layouts: 2.06 us -> 1.72 us
where the time goes in v5:
time: 39.4 us; the launch traced here: 39.3 us
  Pallas kernels  37.6 us (95%)
  local copies, waits for them, and re-layouts  1.72 us (4%)
    pallas_call x1, Pallas kernels, on_device(): pl.pallas_call(kernel, out_shape=jax.ShapeDtypeStruct(signal.shape, BF16)...  37.6 us
    unnamed x3, local copies, waits for them, and re-layouts  1.72 us

profile of v5, /device:TPU:1, one launch (start us, length us, event | category | flops | bytes accessed | tf_op | source)
XLA Modules:
  0.0 39.3 jit_solution(6961025145617935685)
XLA Ops:
  0.0 0.0 copy-start
  0.0 0.8 %copy-done = s32[128,128]{1,0:T(8,128)S(1)} copy-done((s32[128,128]{1,0:T(8,128)S(1)}, s32[128,128]{1,0:T(8,128)}, u32[]{:S(2)}) %copy-start) | copy-done | bytes 65560
  0.8 37.6 %shard_map.37 = bf16[128,3072]{1,0:T(8,128)(2,1)S(1)} custom-call(bf16[128,3072]{1,0:T(8,128)(2,1)} %signal.1, s32[128,128]{1,0:T(8,128)S(1)} %copy-done, bf16[8752,1024]{1,0:T(8,128)(2,1)} %constant.2.clone.table), custom_call_target="tpu_custom_call" | custom-call | flops 5000000000 | bytes 20000000 | tf_op jit(solution)/shard_map/pallas_call | solution.py:357
  38.4 0.9 %copy.5 = bf16[128,3072]{1,0:T(8,128)(2,1)} copy(bf16[128,3072]{1,0:T(8,128)(2,1)S(1)} %shard_map.37) | data formatting | bytes 1572864
Async XLA Ops:
  0.0 0.8 %copy-start = (s32[128,128]{1,0:T(8,128)S(1)}, s32[128,128]{1,0:T(8,128)}, u32[]{:S(2)}) copy-start(s32[128,128]{1,0:T(8,128)} %mask.1) | copy-start | bytes 196612

commit v6 on v5

--- a/solution.py
+++ b/solution.py
@@ -87,7 +87,7 @@
 
 def kernel(
     signal, mask, table, out,
-    sig, mask_v, fwd, inv, packed, taper_v, fine_v, own_part, own_send, other_part, summands,
+    sig, mask_v, fwd, inv, packed, taper_v, fine_v, fan_v, own_part, own_send, other_part, summands,
     send1, got1, send2, got2, kept, leaving, passed, lines_v, frames,
     local, table_sem, sum_send, sum_recv, send_sem, recv1, recv2, pass_send, pass_recv,
 ):
@@ -188,6 +188,27 @@
     def rows(tiles):
         return tiles.reshape(AROUND // 2, ROWS, LINES)
 
+    for copy in small[2:]:
+        copy.wait()
+    for i in range(4):
+        parts = []
+        for k in range(3 * i, 3 * i + 3):
+            top, column = TAPER_ROWS + k // 8 * LINES, k % 8 * LINES
+            parts.append(packed[top : top + LINES, column : column + LINES].astype(F32))
+        fine_v[i] = parts[0] + parts[1] + parts[2]
+    passes = mask_v[pl.ds(me, 1), :].astype(F32) * (1.0 / LINES)
+    cosine, sine = fine_v[2], fine_v[3]
+    left = jnp.concatenate([cosine * passes, sine * passes], axis=1)
+    right = jnp.concatenate(
+        [jnp.concatenate([cosine, sine], axis=1), jnp.concatenate([sine, -cosine], axis=1)], axis=0
+    )
+    fan = jnp.dot(left, right, precision=lax.Precision.HIGHEST, preferred_element_type=F32)
+    fan = jnp.concatenate(
+        [fan, jnp.concatenate([-fan[:, LINES:], fan[:, :LINES]], axis=1)], axis=0
+    )
+    fan_v[0] = fan.astype(BF16)
+    fan_v[1] = (fan - fan.astype(BF16).astype(F32)).astype(BF16)
+
     for pair in range(2):
         for k, layer in enumerate(layers):
             step = pair * LAYERS + k
@@ -205,28 +226,7 @@
             spread(send1, got1, pair, everyone[k], send_sem.at[0], recv1.at[pair])
         got1[pair, here] = send1[pair, here]
 
-    for copy in small[2:]:
-        copy.wait()
-    for i in range(4):
-        parts = []
-        for k in range(3 * i, 3 * i + 3):
-            top, column = TAPER_ROWS + k // 8 * LINES, k % 8 * LINES
-            parts.append(packed[top : top + LINES, column : column + LINES].astype(F32))
-        fine_v[i] = parts[0] + parts[1] + parts[2]
     turns = [packed[PACKED - 2 * LINES :, 2 * LINES * i : 2 * LINES * (i + 1)] for i in range(4)]
-    passes = mask_v[pl.ds(me, 1), :].astype(F32) * (1.0 / LINES)
-    cosine, sine = fine_v[2], fine_v[3]
-    left = jnp.concatenate([cosine * passes, sine * passes], axis=1)
-    right = jnp.concatenate(
-        [jnp.concatenate([cosine, sine], axis=1), jnp.concatenate([sine, -cosine], axis=1)], axis=0
-    )
-    fan = jnp.dot(left, right, precision=lax.Precision.HIGHEST, preferred_element_type=F32)
-    fan = jnp.concatenate(
-        [fan, jnp.concatenate([-fan[:, LINES:], fan[:, :LINES]], axis=1)], axis=0
-    )
-    fan_high = fan.astype(BF16)
-    fan_low = (fan - fan_high.astype(F32)).astype(BF16)
-
     twist_cos, twist_sin = fine_v[0], fine_v[1]
 
     def across_channels(pair):
@@ -258,9 +258,9 @@
         turned = jnp.concatenate(turned, axis=0)
         high = turned.astype(BF16)
         low = (turned - high.astype(F32)).astype(BF16)
-        masked = jnp.dot(high, fan_high, preferred_element_type=F32)
-        masked += jnp.dot(low, fan_high, preferred_element_type=F32)
-        masked += jnp.dot(high, fan_low, preferred_element_type=F32)
+        masked = jnp.dot(high, fan_v[0], preferred_element_type=F32)
+        masked += jnp.dot(low, fan_v[0], preferred_element_type=F32)
+        masked += jnp.dot(high, fan_v[1], preferred_element_type=F32)
         real, imag = [], []
         for b in range(PAIR):
             re = masked[b * LINES : (b + 1) * LINES, :LINES]
@@ -367,6 +367,7 @@
             vmem((PACKED, 2 * BAND), BF16),
             vmem((16, QUARTER), F32),
             vmem((4, LINES, LINES), F32),
+            vmem((2, 2 * LINES, 2 * LINES), BF16),
             vmem((2, *spectra), F32),
             vmem(spectra, BF16),
             vmem((2, *spectra), BF16),

time: 39.4 us -> 39.5 us (level)
  no operation moved by 1% of the time
where the time goes in v6:
time: 39.5 us; the launch traced here: 39.4 us
  Pallas kernels  37.7 us (95%)
  local copies, waits for them, and re-layouts  1.72 us (4%)
    pallas_call x1, Pallas kernels, on_device(): pl.pallas_call(kernel, out_shape=jax.ShapeDtypeStruct(signal.shape, BF16)...  37.7 us
    unnamed x3, local copies, waits for them, and re-layouts  1.72 us

profile of v6, /device:TPU:1, one launch (start us, length us, event | category | flops | bytes accessed | tf_op | source)
XLA Modules:
  0.0 39.4 jit_solution(1694254948446391422)
XLA Ops:
  0.0 0.0 copy-start
  0.0 0.8 %copy-done = s32[128,128]{1,0:T(8,128)S(1)} copy-done((s32[128,128]{1,0:T(8,128)S(1)}, s32[128,128]{1,0:T(8,128)}, u32[]{:S(2)}) %copy-start) | copy-done | bytes 65560
  0.8 37.7 %shard_map.37 = bf16[128,3072]{1,0:T(8,128)(2,1)S(1)} custom-call(bf16[128,3072]{1,0:T(8,128)(2,1)} %signal.1, s32[128,128]{1,0:T(8,128)S(1)} %copy-done, bf16[8752,1024]{1,0:T(8,128)(2,1)} %constant.2.clone.table), custom_call_target="tpu_custom_call" | custom-call | flops 5000000000 | bytes 20000000 | tf_op jit(solution)/shard_map/pallas_call | solution.py:357
  38.5 0.9 %copy.5 = bf16[128,3072]{1,0:T(8,128)(2,1)} copy(bf16[128,3072]{1,0:T(8,128)(2,1)S(1)} %shard_map.37) | data formatting | bytes 1572864
Async XLA Ops:
  0.0 0.8 %copy-start = (s32[128,128]{1,0:T(8,128)S(1)}, s32[128,128]{1,0:T(8,128)}, u32[]{:S(2)}) copy-start(s32[128,128]{1,0:T(8,128)} %mask.1) | copy-start | bytes 196612

commit v7 on v5

--- a/solution.py
+++ b/solution.py
@@ -88,7 +88,7 @@
 def kernel(
     signal, mask, table, out,
     sig, mask_v, fwd, inv, packed, taper_v, fine_v, own_part, own_send, other_part, summands,
-    send1, got1, send2, got2, kept, leaving, passed, lines_v, frames,
+    send1, got1, send2, got2, split, passed, lines_v, frames,
     local, table_sem, sum_send, sum_recv, send_sem, recv1, recv2, pass_send, pass_recv,
 ):
     me, tm = lax.axis_index("chan"), lax.axis_index("tm")
@@ -303,12 +303,11 @@
             tiles = got2[pair, pl.ds(layer * AROUND, AROUND)].astype(F32)
             tiles = tiles.reshape(AROUND // 2, 2, ROWS, LINES)
             low, high = regroup(tiles[:, 0], tiles[:, 1])
-            mine, theirs = jnp.where(x == 0, low, high), jnp.where(x == 0, high, low)
-            kept[pair, layer] = mine.reshape(GROUP, LINES).astype(BF16)
-            leaving[pair, layer] = theirs.reshape(GROUP, LINES).astype(BF16)
-            for kind, source, peer in ((1, leaving, far), (2, leaving, diagonal), (0, kept, partner)):
+            split[0, pair, layer] = low.reshape(GROUP, LINES).astype(BF16)
+            split[1, pair, layer] = high.reshape(GROUP, LINES).astype(BF16)
+            for kind, half, peer in ((1, 1 - x, far), (2, 1 - x, diagonal), (0, x, partner)):
                 pltpu.make_async_remote_copy(
-                    source.at[pair, layer], passed.at[kind, pair, layer], pass_send,
+                    split.at[half, pair, layer], passed.at[kind, pair, layer], pass_send,
                     pass_recv.at[kind, pair], device_id=peer, device_id_type=MESH,
                 ).start()
 
@@ -329,9 +328,9 @@
     for copy in inv_copies:
         copy.wait()
     mine = [i for _, i in places]
-    for k, term in enumerate(terms(kept[0], x, 0, mine)):
+    for k, term in enumerate(terms(split[x, 0], x, 0, mine)):
         frames[k] = term
-    for k, term in enumerate(terms(kept[1], x, 1, mine)):
+    for k, term in enumerate(terms(split[x, 1], x, 1, mine)):
         frames[k] += term
     for k, term in enumerate(terms(arrived(1, 0), 1 - x, 0, mine)):
         frames[k] += term
@@ -375,8 +374,7 @@
             vmem(block, BF16),
             vmem(block, BF16),
             vmem(block, BF16),
-            vmem(spectra, BF16),
-            vmem(spectra, BF16),
+            vmem((2, *spectra), BF16),
             vmem((3, *spectra), BF16),
             vmem((2, PLANE * ROWS, LINES), F32),
             vmem((3, LINES, QUARTER), F32),

time: 39.4 us -> 39.4 us (level)
  no operation moved by 1% of the time
where the time goes in v7:
time: 39.4 us; the launch traced here: 39.3 us
  Pallas kernels  37.6 us (95%)
  local copies, waits for them, and re-layouts  1.72 us (4%)
    pallas_call x1, Pallas kernels, on_device(): pl.pallas_call(kernel, out_shape=jax.ShapeDtypeStruct(signal.shape, BF16)...  37.6 us
    unnamed x3, local copies, waits for them, and re-layouts  1.72 us

profile of v7, /device:TPU:1, one launch (start us, length us, event | category | flops | bytes accessed | tf_op | source)
XLA Modules:
  0.0 39.3 jit_solution(11926204187934384291)
XLA Ops:
  0.0 0.0 copy-start
  0.0 0.8 %copy-done = s32[128,128]{1,0:T(8,128)S(1)} copy-done((s32[128,128]{1,0:T(8,128)S(1)}, s32[128,128]{1,0:T(8,128)}, u32[]{:S(2)}) %copy-start) | copy-done | bytes 65560
  0.8 37.6 %shard_map.37 = bf16[128,3072]{1,0:T(8,128)(2,1)S(1)} custom-call(bf16[128,3072]{1,0:T(8,128)(2,1)} %signal.1, s32[128,128]{1,0:T(8,128)S(1)} %copy-done, bf16[8752,1024]{1,0:T(8,128)(2,1)} %constant.2.clone.table), custom_call_target="tpu_custom_call" | custom-call | flops 5000000000 | bytes 20000000 | tf_op jit(solution)/shard_map/pallas_call | solution.py:356
  38.4 0.9 %copy.5 = bf16[128,3072]{1,0:T(8,128)(2,1)} copy(bf16[128,3072]{1,0:T(8,128)(2,1)S(1)} %shard_map.37) | data formatting | bytes 1572864
Async XLA Ops:
  0.0 0.8 %copy-start = (s32[128,128]{1,0:T(8,128)S(1)}, s32[128,128]{1,0:T(8,128)}, u32[]{:S(2)}) copy-start(s32[128,128]{1,0:T(8,128)} %mask.1) | copy-start | bytes 196612
